TPU v7x, 512 devices: a whole 4x4x16 slice. The times are simulated.
512 devices in a mesh: sec: 16 (over z_hi, y, core), xy: 32 (over z_lo, x).
Axes of the slice: x: 4, y: 4, z: 16 (z_hi: 2, z_lo: 8; z = z_hi * 8 + z_lo), core: 2. Of those that a mesh axis runs over, the one named last changes fastest.
Arguments:
- image: bfloat16 [16, 4096, 512], P('sec', 'xy'), may hold values from -11 to 11
- mask: int32 [16, 4096, 512], P('sec', 'xy'), may hold values from 0 to 1
- flags: int32 [16, 32, 4], P('sec', 'xy'), may hold values 0 or 1
Outputs:
- scores: float32 [16, 32, 4, 1089], P('sec', 'xy')
All inputs are finite; a program needn't handle non-finite values. No bound on the sum of `flags` on one device may be relied on, other than what follows from the above.
Results may differ from a plain program's by a relative error of at most 0.0025.
Values may be sent and summed in bfloat16 or wider, within the bound.
No kernel may reach another device: no remote copies, remote signals or barrier semaphores. Data moves between devices by JAX's collectives and lax.ppermute only.
A program may use at most 64 MiB of HBM per device.

v0:
```python
import jax
import jax.numpy as jnp
from jax import lax
from jax.sharding import PartitionSpec as P

SEARCH = 16
BOX = 8


FLOOR_SHARE = 0.25
EPSILON = 1e-05


def extended_2(block, sides, width):
    for axis, dim in sides:
        count = lax.axis_size(axis)
        forward = [(i, i + 1) for i in range(count - 1)]
        backward = [(target, source) for source, target in forward]
        low = lax.ppermute(
            lax.slice_in_dim(block, block.shape[dim] - width, None, axis=dim), axis, forward
        )
        high = lax.ppermute(lax.slice_in_dim(block, 0, width, axis=dim), axis, backward)
        block = jnp.concatenate([low, block, high], axis=dim)
    return block


def from_behind(block, axis, distance):
    devices = range(lax.axis_size(axis))
    route = [(i - distance, i) for i in devices if i - distance in devices]
    return lax.ppermute(block, axis, route)


def window_sum(values, along_dim, window_len, out_count):
    running = jnp.cumsum(values, axis=along_dim)
    zero_row = jnp.zeros_like(lax.slice_in_dim(values, 0, 1, axis=along_dim))
    running = jnp.concatenate([zero_row, running], axis=along_dim)
    upper = lax.slice_in_dim(running, window_len, window_len + out_count, axis=along_dim)
    lower = lax.slice_in_dim(running, 0, out_count, axis=along_dim)
    return upper - lower


def normalize(raw_padded, tissue, box_half, window_tool):
    row_count, col_count = tissue.shape
    padded = jnp.pad(raw_padded, ((0, 0), (box_half, box_half)))
    side_len = 2 * box_half + 1

    def local_average(values):
        across_sum = window_tool(values, 1, side_len, col_count)
        return window_tool(across_sum, 0, side_len, row_count) / float(side_len * side_len)

    local_mean = local_average(padded)
    local_square = local_average(padded * padded)
    centre = raw_padded[box_half : box_half + row_count]
    scaled = (centre - local_mean) * lax.rsqrt(local_square - local_mean * local_mean + EPSILON)
    return (tissue.astype(jnp.float32) * scaled).astype(jnp.bfloat16)


def windows_of(extended, patch_len, col_count, span_len):
    widened = jnp.pad(extended, ((0, 0), (0, patch_len - span_len + 1)))
    main_part = widened[:, : col_count * patch_len].reshape(-1, col_count, patch_len)
    tail_part = widened[:, patch_len : (col_count + 1) * patch_len].reshape(
        -1, col_count, patch_len
    )[:, :, : span_len - 1]
    return jnp.concatenate([main_part, tail_part], axis=2)


def shear_sum(product, span_len):
    lead_shape = product.shape[:-2]
    patch_len = product.shape[-2]
    wide_len = product.shape[-1]
    flattened = product.reshape(lead_shape + (patch_len * wide_len,))
    flattened = jnp.pad(flattened, [(0, 0)] * len(lead_shape) + [(0, patch_len)])
    sheared = flattened.reshape(lead_shape + (patch_len, wide_len + 1))
    return jnp.sum(sheared[..., :span_len], axis=-2)


def strip_scores(own_strip, extended, validity, span_len):
    patch_len = own_strip.shape[0]
    col_count = own_strip.shape[1] // patch_len
    patches = own_strip.reshape(patch_len, col_count, patch_len)
    windows = windows_of(extended, patch_len, col_count, span_len)
    group_len = 3

    def one_group(group_index):
        slabs = jnp.stack(
            [
                lax.dynamic_slice_in_dim(windows, group_index * group_len + offset, patch_len, 0)
                for offset in range(group_len)
            ]
        )
        product = jnp.einsum("ypx,uypc->upxc", patches, slabs, preferred_element_type=jnp.float32)
        return shear_sum(product, span_len)

    numerator = lax.map(one_group, jnp.arange(span_len // group_len, dtype=jnp.int32))
    numerator = numerator.reshape(span_len, col_count, span_len)
    squares = windows.astype(jnp.float32)
    squares = squares * squares
    energy_next = window_sum(window_sum(squares, 0, patch_len, span_len), 2, patch_len, span_len)
    own_values = patches.astype(jnp.float32)
    energy_own = jnp.sum(own_values * own_values, axis=(0, 2))
    floor_value = FLOOR_SHARE * patch_len * patch_len
    denominator = jnp.sqrt(
        jnp.maximum(energy_own, floor_value)[None, :, None] * jnp.maximum(energy_next, floor_value)
    )
    ratio = validity.astype(jnp.float32)[None, :, None] * numerator / denominator
    return jnp.transpose(ratio, (1, 0, 2)).reshape(col_count, span_len * span_len)


def shards(image, mask, flags):
    span_len = 2 * SEARCH + 1
    raw_rows = extended_2(image[0], (("xy", 0),), BOX)
    own_strip = normalize(raw_rows.astype(jnp.float32), mask[0], BOX, window_sum)
    following = from_behind(own_strip, "sec", -1)
    extended = extended_2(following, (("xy", 0),), SEARCH)
    extended = jnp.pad(extended, ((0, 0), (SEARCH, SEARCH)))
    scores = strip_scores(own_strip, extended, flags[0, 0], span_len)
    return scores.reshape(1, 1, scores.shape[0], scores.shape[1])


def solution(mesh):
    placed = (P("sec", "xy", None), P("sec", "xy", None), P("sec", "xy", None))
    return jax.shard_map(
        shards, mesh=mesh, in_specs=placed, out_specs=P("sec", "xy", None, None), check_vma=False
    )
```

profile of v0, /device:TPU:57, one launch (start us, length us, event | category | flops | bytes accessed | tf_op | source)
XLA Modules:
  0.0 237.3 jit_solution(14554359407114603313)
XLA Ops:
  0.7 3.9 %collective-permute-start.1 = (bf16[8,512]{1,0:T(8,128)(2,1)S(1)}, bf16[8,512]{1,0:T(8,128)(2,1)S(1)}, u32[]{:S(2)}, u32[]{:S(2)}) collective-permute-start(bf16[8,512]{1,0:T(8,128)(2,1)S(1)} %get-tuple-element.105), channel_id=1, source_target_pairs={{1,0},{2,1},{3,2},{4,3},{5,4},{6,5},{7,6},{8,7},{9,8},{10,9},{11,1... | collective-permute-start | bytes 24584 | tf_op jit(solution)/shard_map/ppermute | solution.py:22
  4.6 1.9 collective-permute-start
  6.6 4.6 %collective-permute-done = bf16[8,512]{1,0:T(8,128)(2,1)S(1)} collective-permute-done((bf16[8,512]{1,0:T(8,128)(2,1)S(1)}, bf16[8,512]{1,0:T(8,128)(2,1)S(1)}, u32[]{:S(2)}, u32[]{:S(2)}) %collective-permute-start) | collective-permute-done | bytes 8224 | tf_op jit(solution)/shard_map/ppermute | solution.py:19
  12.9 56.3 %fusion.43 = f32[144,5,128]{0,1,2:T(8,128)S(1)} fusion(f32[144,5,128]{0,1,2:T(8,128)S(1)} %copy.34), kind=kOutput, calls=%fused_computation.84 | output fusion | flops 11704320 | bytes 737280 | tf_op jit(solution)/shard_map/reduce-window.4
  72.2 56.3 %fusion.42 = f32[144,5,128]{0,1,2:T(8,128)S(1)} fusion(f32[144,5,128]{0,1,2:T(8,128)S(1)} %copy.30), kind=kOutput, calls=%fused_computation.83 | output fusion | flops 11704320 | bytes 737280 | tf_op jit(solution)/shard_map/reduce-window
  131.2 4.0 %collective-permute-start.2 = (bf16[128,512]{1,0:T(8,128)(2,1)S(1)}, bf16[128,512]{1,0:T(8,128)(2,1)S(1)}, u32[]{:S(2)}, u32[]{:S(2)}) collective-permute-start(bf16[128,512]{1,0:T(8,128)(2,1)S(1)} %get-tuple-element.94), channel_id=1, source_target_pairs={{32,0},{64,32},{96,64},{128,96},{160,128},{192,160},{224,192},{256... | collective-permute-start | bytes 393224 | tf_op jit(solution)/shard_map/ppermute | solution.py:30
  135.3 17.1 %collective-permute-done.2 = bf16[128,512]{1,0:T(8,128)(2,1)S(1)} collective-permute-done((bf16[128,512]{1,0:T(8,128)(2,1)S(1)}, bf16[128,512]{1,0:T(8,128)(2,1)S(1)}, u32[]{:S(2)}, u32[]{:S(2)}) %collective-permute-start.2) | collective-permute-done | bytes 131104 | tf_op jit(solution)/shard_map/ppermute | solution.py:30
  152.4 1.9 collective-permute-start.4
  154.3 3.5 %collective-permute-start.3 = (bf16[16,512]{1,0:T(8,128)(2,1)S(1)}, bf16[16,512]{1,0:T(8,128)(2,1)S(1)}, u32[]{:S(2)}, u32[]{:S(2)}) collective-permute-start(bf16[16,512]{1,0:T(8,128)(2,1)S(1)} %get-tuple-element.102), channel_id=1, source_target_pairs={{0,1},{1,2},{2,3},{3,4},{4,5},{5,6},{6,7},{7,8},{8,9},{9,10},{10,1... | collective-permute-start | bytes 49160 | tf_op jit(solution)/shard_map/ppermute | solution.py:19
  158.2 2.8 %collective-permute-done.3 = bf16[16,512]{1,0:T(8,128)(2,1)S(1)} collective-permute-done((bf16[16,512]{1,0:T(8,128)(2,1)S(1)}, bf16[16,512]{1,0:T(8,128)(2,1)S(1)}, u32[]{:S(2)}, u32[]{:S(2)}) %collective-permute-start.3) | collective-permute-done | bytes 16416 | tf_op jit(solution)/shard_map/ppermute | solution.py:19
  161.6 1.2 reshape.111
  162.7 2.4 %copy.42 = f32[160,4,2,128]{0,2,1,3:T(2,128)S(1)} copy(f32[160,4,2,128]{3,2,0,1:T(2,128)} %reshape.111) | data formatting | bytes 1310720 | tf_op jit(solution)/shard_map/reshape.18
  165.6 1.9 copy.43
  167.5 1.6 reduce_window_sum.89
  169.6 2.3 reduce-window.56
  172.3 64.1 %while.12 = (s32[]{:T(128)}, f32[11,3,4,33]{3,2,1,0:T(4,128)S(1)}, s32[11]{0:T(128)S(1)}, bf16[160,4,160]{0,2,1:T(8,128)(2,1)S(1)}, bf16[128,4,128]{2,0,1:T(8,12...) while((s32[]{:T(128)}, f32[11,3,4,33]{3,2,1,0:T(4,128)S(1)}, ...), condition=%wide.region_10.11_spmd, body=%wide.region_8.10_spmd.sunk | while | flops 63456384 | bytes 10688351 | solution.py:94
  174.7 1.1 reshape.119
  176.0 2.0 reshape.120
  180.5 1.1 reshape.119
  181.9 2.0 reshape.120
  186.4 1.1 reshape.119
  187.7 2.0 reshape.120
  192.2 1.1 reshape.119
  193.5 2.0 reshape.120
  198.0 1.1 reshape.119
  199.4 2.0 reshape.120
  205.2 2.0 reshape.120
  211.0 2.0 reshape.120
  216.8 2.0 reshape.120
  222.7 2.0 reshape.120
  228.5 2.0 reshape.120
  234.3 2.0 reshape.120
  (163 shorter events, 38.9 us)
Async XLA Ops:
  0.7 5.9 %collective-permute-start.1 = (bf16[8,512]{1,0:T(8,128)(2,1)S(1)}, bf16[8,512]{1,0:T(8,128)(2,1)S(1)}, u32[]{:S(2)}, u32[]{:S(2)}) collective-permute-start(bf16[8,512]{1,0:T(8,128)(2,1)S(1)} %get-tuple-element.105), channel_id=1, source_target_pairs={{1,0},{2,1},{3,2},{4,3},{5,4},{6,5},{7,6},{8,7},{9,8},{10,9},{11,1... | collective-permute-start | bytes 24584 | tf_op jit(solution)/shard_map/ppermute | solution.py:22
  4.6 6.5 %collective-permute-start = (bf16[8,512]{1,0:T(8,128)(2,1)S(1)}, bf16[8,512]{1,0:T(8,128)(2,1)S(1)}, u32[]{:S(2)}, u32[]{:S(2)}) collective-permute-start(bf16[8,512]{1,0:T(8,128)(2,1)S(1)} %get-tuple-element.104), channel_id=1, source_target_pairs={{0,1},{1,2},{2,3},{3,4},{4,5},{5,6},{6,7},{7,8},{8,9},{9,10},{10,1... | collective-permute-start | bytes 24584 | tf_op jit(solution)/shard_map/ppermute | solution.py:19
  129.9 1.0 copy-start
  129.9 1.0 copy-start.1
  130.0 5.1 %copy-start.2 = (s32[1,1,4]{2,1,0:T(1,128)S(1)}, s32[1,1,4]{2,1,0:T(1,128)}, u32[]{:S(2)}) copy-start(s32[1,1,4]{2,1,0:T(1,128)} %param.7) | copy-start | bytes 52
  131.2 21.2 %collective-permute-start.2 = (bf16[128,512]{1,0:T(8,128)(2,1)S(1)}, bf16[128,512]{1,0:T(8,128)(2,1)S(1)}, u32[]{:S(2)}, u32[]{:S(2)}) collective-permute-start(bf16[128,512]{1,0:T(8,128)(2,1)S(1)} %get-tuple-element.94), channel_id=1, source_target_pairs={{32,0},{64,32},{96,64},{128,96},{160,128},{192,160},{224,192},{256... | collective-permute-start | bytes 393224 | tf_op jit(solution)/shard_map/ppermute | solution.py:30
  152.4 5.7 %collective-permute-start.4 = (bf16[16,512]{1,0:T(8,128)(2,1)S(1)}, bf16[16,512]{1,0:T(8,128)(2,1)S(1)}, u32[]{:S(2)}, u32[]{:S(2)}) collective-permute-start(bf16[16,512]{1,0:T(8,128)(2,1)S(1)} %get-tuple-element.103), channel_id=1, source_target_pairs={{1,0},{2,1},{3,2},{4,3},{5,4},{6,5},{7,6},{8,7},{9,8},{10,9},{11,1... | collective-permute-start | bytes 49160 | tf_op jit(solution)/shard_map/ppermute | solution.py:22
  154.3 6.6 %collective-permute-start.3 = (bf16[16,512]{1,0:T(8,128)(2,1)S(1)}, bf16[16,512]{1,0:T(8,128)(2,1)S(1)}, u32[]{:S(2)}, u32[]{:S(2)}) collective-permute-start(bf16[16,512]{1,0:T(8,128)(2,1)S(1)} %get-tuple-element.102), channel_id=1, source_target_pairs={{0,1},{1,2},{2,3},{3,4},{4,5},{5,6},{6,7},{7,8},{8,9},{9,10},{10,1... | collective-permute-start | bytes 49160 | tf_op jit(solution)/shard_map/ppermute | solution.py:19
where the time goes:
time: 238 us; the launch traced here: 237 us
  other arithmetic  120 us (50%)
  local copies, waits for them, and re-layouts  65.5 us (28%)
  waiting for transfers between devices  24.4 us (10%)
  starting transfers between devices  15.3 us (6%)
  loops' own time  8.44 us (4%)
  matrix products  3.02 us (1%)
    another operation x20, other arithmetic  117 us
    reshape x11, local copies, waits for them, and re-layouts, shear_sum(): sheared = flattened.reshape(lead_shape + (patch_len, wide_len + 1))  22.1 us
    ppermute x1, waiting for transfers between devices, from_behind(): return lax.ppermute(block, axis, route)  17.1 us
    reshape x11, local copies, waits for them, and re-layouts, shear_sum(): flattened = product.reshape(lead_shape + (patch_len * wide_len,))  12.5 us
    another operation x30, local copies, waits for them, and re-layouts  10.3 us
    another operation x1, loops' own time, strip_scores(): lax.map(one_group, jnp.arange(span_len // group_len, dtype=jnp.int32))  8.44 us
    dynamic_slice x11, local copies, waits for them, and re-layouts, strip_scores(): lax.map(one_group, jnp.arange(span_len // group_len, dtype=jnp.int32))  7.33 us
    ppermute x2, waiting for transfers between devices, extended_2(): lax.ppermute(lax.slice_in_dim(block, block.shape[dim] - width, None, axis...  7.32 us
  transfers between devices with their start and end apart: 5, of which 3 were waited for; matrix products, arithmetic and copies ran while one was open for 0% of the time, Pallas kernels for 0%

commit v1 on v0

v1 whole, which is shorter than its diff:
```python
import jax
import jax.numpy as jnp
from jax import lax
from jax.experimental import pallas as pl
from jax.experimental.pallas import tpu as pltpu
from jax.sharding import PartitionSpec as P

PATCH = 128
SEARCH = 16
BOX = 8
SPAN = 2 * SEARCH + 1
SIDE = 2 * BOX + 1
PCOL = 4
W = PCOL * PATCH
EXT = PATCH + 2 * SEARCH
GROUP = 32
JN = PATCH // GROUP
FLOOR_SHARE = 0.25
EPSILON = 1e-05
F32 = jnp.float32
BF16 = jnp.bfloat16


def iota(shape, dim):
    return lax.broadcasted_iota(jnp.int32, shape, dim)


def mm(a, b):
    return jnp.dot(a, b, preferred_element_type=F32)


def band():
    r, c = iota((W, W // 2), 0), iota((W, W // 2), 1)
    return jnp.where(jnp.abs(r - PATCH - c) <= BOX, 1.0, 0.0).astype(BF16)


def across(x, g):
    lo = mm(x[:, : 3 * PATCH], g[PATCH:])
    hi = mm(x[:, PATCH:], g[: 3 * PATCH])
    return jnp.concatenate([lo, hi], axis=1)


def down(s, rows):
    n = rows + SIDE - 1
    s2 = s[: n - 1] + s[1:]
    s4 = s2[: n - 3] + s2[2:]
    s8 = s4[: n - 7] + s4[4:]
    s16 = s8[: n - 15] + s8[8:]
    return s16[:rows] + s[SIDE - 1 : SIDE - 1 + rows]


def normalized(x, tissue, g):
    rows = tissue.shape[0]
    xf = x.astype(F32)
    sq = xf * xf
    sq_hi = sq.astype(BF16)
    sq_lo = (sq - sq_hi.astype(F32)).astype(BF16)
    area = 1.0 / float(SIDE * SIDE)
    mean = down(across(x, g), rows) * area
    square = down(across(sq_hi, g) + across(sq_lo, g), rows) * area
    var = jnp.maximum(square - mean * mean, 0.0)
    scaled = (xf[BOX : BOX + rows] - mean) * lax.rsqrt(var + EPSILON)
    return (tissue * scaled).astype(BF16)


def correlate(a, b, flags_ref, out_ref, bpad, wgt, lhs, prod):
    r, c = iota((PATCH, PATCH), 0), iota((PATCH, PATCH), 1)
    flip = jnp.where((r // GROUP) * GROUP + (GROUP - 1 - r % GROUP) == c, 1.0, 0.0).astype(BF16)
    turned = [
        lax.dot_general(
            flip, a[:, PATCH * p : PATCH * (p + 1)], (((1,), (1,)), ((), ())), preferred_element_type=F32
        )
        for p in range(PCOL)
    ]
    bpad[...] = jnp.zeros_like(bpad)
    bpad[:, SEARCH : SEARCH + W] = b.astype(F32)
    wgt[...] = jnp.zeros_like(wgt)
    for j in range(JN):
        for p in range(PCOL):
            at = PATCH * p + GROUP * j
            wgt[pl.ds(j * PCOL * EXT + p * EXT, EXT), pl.ds(64 * p, 64)] = bpad[:, at : at + 64].astype(BF16)
    lane = iota((PATCH, PATCH), 1)
    tiles = PCOL * EXT // PATCH
    for u in range(SPAN):
        parts = [None] * (tiles + 1)
        for p in range(PCOL):
            t, o = divmod(EXT * p + u, PATCH)
            moved = pltpu.roll(turned[p], o, 1) if o else turned[p]
            for tile, keep in ((t, lane >= o), (t + 1, lane < o)):
                if tile == t + 1 and o == 0:
                    continue
                base = parts[tile]
                parts[tile] = jnp.where(keep, moved, 0.0 if base is None else base)
        for tile in range(tiles):
            val = parts[tile].astype(BF16)
            for j in range(JN):
                lhs[pl.ds(u * GROUP, GROUP), pl.ds((j * tiles + tile) * PATCH, PATCH)] = val[GROUP * j : GROUP * (j + 1)]
    prod[...] = mm(lhs[...], wgt[...])
    rows = []
    pieces = []
    for h in range(2):
        block = prod[:, pl.ds(PATCH * h, PATCH)].reshape(SPAN, JN, 8, PATCH)
        total = None
        for q in range(GROUP // 8):
            part = block[:, q].reshape(SPAN * 8, PATCH)
            part = part.reshape(SPAN, 8, PATCH)
            moved = pltpu.roll(part, PATCH - (GROUP - 1) + 8 * q, 2, stride=1, stride_axis=1)
            total = moved if total is None else total + moved
        pieces.append(jnp.sum(total, axis=1))
    numer = jnp.concatenate(pieces, axis=1)
    bf = b.astype(F32)
    sq = bf * bf
    sq_hi = sq.astype(BF16)
    sq_lo = (sq - sq_hi.astype(F32)).astype(BF16)
    ur, uc = iota((40, EXT), 0), iota((40, EXT), 1)
    vert = jnp.where((uc >= ur) & (uc < ur + PATCH), 1.0, 0.0).astype(BF16)
    col = mm(vert, sq_hi) + mm(vert, sq_lo)
    col_hi = col.astype(BF16)
    col_lo = (col - col_hi.astype(F32)).astype(BF16)
    xr, xc = iota((W, 64 * PCOL), 0), iota((W, 64 * PCOL), 1)
    start = (xc // 64) * PATCH + (xc % 64) - SEARCH
    horiz = jnp.where((xr >= start) & (xr < start + PATCH), 1.0, 0.0).astype(BF16)
    energy_next = (mm(col_hi, horiz) + mm(col_lo, horiz))[:SPAN]
    af = a.astype(F32)
    own = jnp.sum(af * af, axis=0, keepdims=True)
    own_hi = own.astype(BF16)
    own_lo = (own - own_hi.astype(F32)).astype(BF16)
    same = jnp.where(xr // PATCH == xc // 64, 1.0, 0.0).astype(BF16)
    own8 = jnp.concatenate([own_hi, own_lo, jnp.zeros((14, W), BF16)], axis=0)
    own_sum = mm(own8, same)
    energy_own = own_sum[0:1] + own_sum[1:2]
    floor_value = FLOOR_SHARE * PATCH * PATCH
    scale = lax.rsqrt(jnp.maximum(energy_own, floor_value)) * lax.rsqrt(jnp.maximum(energy_next, floor_value))
    score = numer * scale
    score = jnp.concatenate([score, jnp.zeros((40 - SPAN, 64 * PCOL), F32)], axis=0)
    ur, lane = iota((40, PATCH), 0), iota((40, PATCH), 1)
    for h in range(2):
        half = score[:, PATCH * h : PATCH * (h + 1)]
        for s in range(2):
            p = 2 * h + s
            flag = flags_ref[p].astype(F32)
            lines = []
            for k in range(5):
                rows8 = (half * flag)[8 * k : 8 * k + 8]
                base = (8 * k - 64 * s) % PATCH
                rows8 = pltpu.roll(rows8, base, 1) if base else rows8
                rows8 = pltpu.roll(rows8, 0, 1, stride=16, stride_axis=0)
                lines.append(pltpu.roll(rows8, 0, 1, stride=17, stride_axis=0))
            moved = jnp.concatenate(lines, axis=0)
            for t in range(9):
                at = t * PATCH + lane
                pick = (at >= SPAN * ur) & (at < SPAN * ur + SPAN)
                line = jnp.sum(jnp.where(pick, moved, 0.0), axis=0, keepdims=True)
                wide = min(PATCH, SPAN * SPAN - t * PATCH)
                out_ref[p : p + 1, t * PATCH : t * PATCH + wide] = line[:, :wide]


VMEM = pl.BlockSpec(memory_space=pltpu.VMEM)
SMEM = pl.BlockSpec(memory_space=pltpu.SMEM)
HALO = 32


def normalize_body(low_ref, mid_ref, high_ref, tissue_ref, out_ref):
    low, high = low_ref[...], high_ref[...]
    x = jnp.concatenate([low[SEARCH - BOX : HALO], mid_ref[...], high[: HALO - (SEARCH - BOX)]], axis=0)
    tissue = jnp.concatenate(
        [low[HALO:].astype(F32), tissue_ref[...].astype(F32), high[HALO:].astype(F32)], axis=0
    )
    out_ref[...] = normalized(x, tissue, band())


def correlate_body(own_ref, next_ref, flags_ref, out_ref, *scratch):
    correlate(own_ref[SEARCH : SEARCH + PATCH], next_ref[...], flags_ref, out_ref, *scratch)


def halo(image, tissue, top):
    if top:
        return jnp.concatenate([image[:HALO], tissue[:SEARCH].astype(BF16)], axis=0)
    return jnp.concatenate([image[-HALO:], tissue[-SEARCH:].astype(BF16)], axis=0)


def shards(image, mask, flags):
    image, mask, flags = image[0], mask[0], flags[0, 0]
    count = lax.axis_size("xy")
    forward = [(i, i + 1) for i in range(count - 1)]
    backward = [(b, a) for a, b in forward]
    low = lax.ppermute(halo(image, mask, False), "xy", forward)
    high = lax.ppermute(halo(image, mask, True), "xy", backward)
    own = pl.pallas_call(
        normalize_body,
        out_shape=jax.ShapeDtypeStruct((EXT, W), BF16),
        in_specs=[VMEM] * 4,
        out_specs=VMEM,
        compiler_params=pltpu.CompilerParams(vmem_limit_bytes=48 << 20),
    )(low, image, high, mask)
    sections = lax.axis_size("sec")
    following = lax.ppermute(own, "sec", [(s + 1, s) for s in range(sections - 1)])
    scores = pl.pallas_call(
        correlate_body,
        out_shape=jax.ShapeDtypeStruct((PCOL, SPAN * SPAN), F32),
        in_specs=[VMEM, VMEM, SMEM],
        out_specs=VMEM,
        scratch_shapes=[
            pltpu.VMEM((EXT, W + PATCH), F32),
            pltpu.VMEM((JN * PCOL * EXT, 64 * PCOL), BF16),
            pltpu.VMEM((SPAN * GROUP, JN * PCOL * EXT), BF16),
            pltpu.VMEM((SPAN * GROUP, 64 * PCOL), F32),
        ],
        compiler_params=pltpu.CompilerParams(vmem_limit_bytes=48 << 20),
    )(own, following, flags)
    return scores[None, None]


def solution(mesh):
    placed = (P("sec", "xy", None), P("sec", "xy", None), P("sec", "xy", None))
    return jax.shard_map(
        shards, mesh=mesh, in_specs=placed, out_specs=P("sec", "xy", None, None), check_vma=False
    )
```

time: 238 us -> 41.4 us (0.17)
  the two profiles are of different devices: /device:TPU:57 before, /device:TPU:127 now
where the time goes in v1:
time: 41.4 us; the launch traced here: 41.1 us
  waiting for transfers between devices  23.2 us (56%)
  starting transfers between devices  10.7 us (26%)
  Pallas kernels  5.28 us (13%)
  other arithmetic  1.05 us (3%)
  local copies, waits for them, and re-layouts  0.8 us (2%)
    ppermute x1, waiting for transfers between devices, shards(): lax.ppermute(own, 'sec', [(s + 1, s) for s in range(sections - 1)])  17 us
    ppermute x1, waiting for transfers between devices, shards(): high = lax.ppermute(halo(image, mask, True), 'xy', backward)  6.22 us
    ppermute x1, starting transfers between devices, shards(): low = lax.ppermute(halo(image, mask, False), 'xy', forward)  4.8 us
    pallas_call x1, Pallas kernels, shards(): pl.pallas_call(correlate_body, out_shape=jax.ShapeDtypeStruct((PCOL, SPAN...  4.47 us
    ppermute x1, starting transfers between devices, shards(): lax.ppermute(own, 'sec', [(s + 1, s) for s in range(sections - 1)])  4.01 us
    ppermute x1, starting transfers between devices, shards(): high = lax.ppermute(halo(image, mask, True), 'xy', backward)  1.92 us
    another operation x1, other arithmetic  1.04 us
  transfers between devices with their start and end apart: 3, of which 2 were waited for; matrix products, arithmetic and copies ran while one was open for 0% of the time, Pallas kernels for 0%

profile of v1, /device:TPU:127, one launch (start us, length us, event | category | flops | bytes accessed | tf_op | source)
XLA Modules:
  0.0 41.1 jit_solution(8681688850224238687)
XLA Ops:
  0.0 0.8 %slice_bitcast_fusion = (bf16[32,512]{1,0:T(8,128)(2,1)S(1)}, bf16[32,512]{1,0:T(8,128)(2,1)S(1)}) fusion(bf16[1,128,512]{2,1,0:T(8,128)(2,1)} %param.3), kind=kLoop, calls=%fused_computation.2 | loop fusion | bytes 131072 | tf_op jit(solution)/shard_map/slice | solution.py:178
  0.8 0.0 copy-start
  0.8 1.0 %convert.4 = bf16[1,128,512]{2,1,0:T(8,128)(2,1)S(1)} convert(s32[1,128,512]{2,1,0:T(8,128)} %param.4) | non-fusion elementwise | flops 65536 | bytes 393216 | tf_op jit(solution)/shard_map/convert.1
  1.8 0.0 copy-start.1
  1.9 4.8 %collective-permute-start = (bf16[48,512]{1,0:T(8,128)(2,1)S(1)}, bf16[48,512]{1,0:T(8,128)(2,1)S(1)}, u32[]{:S(2)}, u32[]{:S(2)}) collective-permute-start(bf16[48,512]{1,0:T(8,128)(2,1)S(1)} %pad_maximum_fusion), channel_id=1, source_target_pairs={{0,1},{1,2},{2,3},{3,4},{4,5},{5,6},{6,7},{7,8},{8,9},{9,10},{10,1... | collective-permute-start | bytes 147464 | tf_op jit(solution)/shard_map/ppermute | solution.py:187
  6.7 1.9 %collective-permute-start.1 = (bf16[48,512]{1,0:T(8,128)(2,1)S(1)}, bf16[48,512]{1,0:T(8,128)(2,1)S(1)}, u32[]{:S(2)}, u32[]{:S(2)}) collective-permute-start(bf16[48,512]{1,0:T(8,128)(2,1)S(1)} %pad_maximum_fusion.1), channel_id=1, source_target_pairs={{1,0},{2,1},{3,2},{4,3},{5,4},{6,5},{7,6},{8,7},{9,8},{10,9},{11,1... | collective-permute-start | bytes 147464 | tf_op jit(solution)/shard_map/ppermute | solution.py:188
  8.6 0.0 collective-permute-done.low_ref
  8.6 6.2 %collective-permute-done.1.high_ref = bf16[48,512]{1,0:T(8,128)(2,1)S(1)} collective-permute-done((bf16[48,512]{1,0:T(8,128)(2,1)S(1)}, bf16[48,512]{1,0:T(8,128)(2,1)S(1)}, u32[]{:S(2)}, u32[]{:S(2)}) %collective-permute-start.1) | collective-permute-done | bytes 49184 | tf_op jit(solution)/shard_map/ppermute | solution.py:188
  14.8 0.0 copy-done
  14.8 0.0 copy-done.1
  14.8 0.8 %shard_map.37.own_ref = bf16[160,512]{1,0:T(8,128)(2,1)S(1)} custom-call(bf16[48,512]{1,0:T(8,128)(2,1)S(1)} %collective-permute-done.low_ref, bf16[128,512]{1,0:T(8,128)(2,1)S(1)} %bitcast.13, bf16[48,512]{1,0:T(8,128)(2,1)S(1)} %collective-permute-done.1.high_ref, s32[128,512]{1,0:T(8,128)S(1)} %bitcast.12), custom_call_target="tpu_custom_call" | custom-call | tf_op jit(solution)/shard_map/pallas_call | solution.py:189
  15.7 0.0 copy-start.2
  15.7 4.0 %collective-permute-start.2 = (bf16[160,512]{1,0:T(8,128)(2,1)S(1)}, bf16[160,512]{1,0:T(8,128)(2,1)S(1)}, u32[]{:S(2)}, u32[]{:S(2)}) collective-permute-start(bf16[160,512]{1,0:T(8,128)(2,1)S(1)} %shard_map.37.own_ref), channel_id=1, source_target_pairs={{32,0},{64,32},{96,64},{128,96},{160,128},{192,160},{224,192},{256... | collective-permute-start | bytes 491528 | tf_op jit(solution)/shard_map/ppermute | solution.py:197
  19.7 17.0 %collective-permute-done.2.next_ref = bf16[160,512]{1,0:T(8,128)(2,1)S(1)} collective-permute-done((bf16[160,512]{1,0:T(8,128)(2,1)S(1)}, bf16[160,512]{1,0:T(8,128)(2,1)S(1)}, u32[]{:S(2)}, u32[]{:S(2)}) %collective-permute-start.2) | collective-permute-done | bytes 163872 | tf_op jit(solution)/shard_map/ppermute | solution.py:197
  36.6 0.0 copy-done.2
  36.7 4.5 %shard_map.38 = f32[4,1089]{1,0:T(4,128)} custom-call(bf16[160,512]{1,0:T(8,128)(2,1)S(1)} %shard_map.37.own_ref, bf16[160,512]{1,0:T(8,128)(2,1)S(1)} %collective-permute-done.2.next_ref, s32[4]{0:T(128)S(1)} %bitcast.14), custom_call_target="tpu_custom_call" | custom-call | tf_op jit(solution)/shard_map/pallas_call | solution.py:198
  (3 shorter events, 0.0 us)
Async XLA Ops:
  0.8 14.1 %copy-start = (s32[1,128,512]{2,1,0:T(8,128)S(1)}, s32[1,128,512]{2,1,0:T(8,128)}, u32[]{:S(2)}) copy-start(s32[1,128,512]{2,1,0:T(8,128)} %param.4) | copy-start | bytes 786436
  1.8 13.0 %copy-start.1 = (bf16[1,128,512]{2,1,0:T(8,128)(2,1)S(1)}, bf16[1,128,512]{2,1,0:T(8,128)(2,1)}, u32[]{:S(2)}) copy-start(bf16[1,128,512]{2,1,0:T(8,128)(2,1)} %param.3) | copy-start | bytes 393220
  1.9 6.8 %collective-permute-start = (bf16[48,512]{1,0:T(8,128)(2,1)S(1)}, bf16[48,512]{1,0:T(8,128)(2,1)S(1)}, u32[]{:S(2)}, u32[]{:S(2)}) collective-permute-start(bf16[48,512]{1,0:T(8,128)(2,1)S(1)} %pad_maximum_fusion), channel_id=1, source_target_pairs={{0,1},{1,2},{2,3},{3,4},{4,5},{5,6},{6,7},{7,8},{8,9},{9,10},{10,1... | collective-permute-start | bytes 147464 | tf_op jit(solution)/shard_map/ppermute | solution.py:187
  6.7 8.2 %collective-permute-start.1 = (bf16[48,512]{1,0:T(8,128)(2,1)S(1)}, bf16[48,512]{1,0:T(8,128)(2,1)S(1)}, u32[]{:S(2)}, u32[]{:S(2)}) collective-permute-start(bf16[48,512]{1,0:T(8,128)(2,1)S(1)} %pad_maximum_fusion.1), channel_id=1, source_target_pairs={{1,0},{2,1},{3,2},{4,3},{5,4},{6,5},{7,6},{8,7},{9,8},{10,9},{11,1... | collective-permute-start | bytes 147464 | tf_op jit(solution)/shard_map/ppermute | solution.py:188
  15.7 21.0 %copy-start.2 = (s32[1,1,4]{2,1,0:T(1,128)S(1)}, s32[1,1,4]{2,1,0:T(1,128)}, u32[]{:S(2)}) copy-start(s32[1,1,4]{2,1,0:T(1,128)} %param.5) | copy-start | bytes 52
  15.7 21.0 %collective-permute-start.2 = (bf16[160,512]{1,0:T(8,128)(2,1)S(1)}, bf16[160,512]{1,0:T(8,128)(2,1)S(1)}, u32[]{:S(2)}, u32[]{:S(2)}) collective-permute-start(bf16[160,512]{1,0:T(8,128)(2,1)S(1)} %shard_map.37.own_ref), channel_id=1, source_target_pairs={{32,0},{64,32},{96,64},{128,96},{160,128},{192,160},{224,192},{256... | collective-permute-start | bytes 491528 | tf_op jit(solution)/shard_map/ppermute | solution.py:197

commit v2 on v1

--- a/solution.py
+++ b/solution.py
@@ -15,7 +15,7 @@
 EXT = PATCH + 2 * SEARCH
 GROUP = 32
 JN = PATCH // GROUP
-FLOOR_SHARE = 0.25
+FLOOR = 0.25 * PATCH * PATCH
 EPSILON = 1e-05
 F32 = jnp.float32
 BF16 = jnp.bfloat16
@@ -51,7 +51,8 @@
 
 def normalized(x, tissue, g):
     rows = tissue.shape[0]
-    xf = x.astype(F32)
+    xf = x
+    x = xf.astype(BF16)
     sq = xf * xf
     sq_hi = sq.astype(BF16)
     sq_lo = (sq - sq_hi.astype(F32)).astype(BF16)
@@ -63,7 +64,7 @@
     return (tissue * scaled).astype(BF16)
 
 
-def correlate(a, b, flags_ref, out_ref, bpad, wgt, lhs, prod):
+def shifted(a, lhs, own_scale):
     r, c = iota((PATCH, PATCH), 0), iota((PATCH, PATCH), 1)
     flip = jnp.where((r // GROUP) * GROUP + (GROUP - 1 - r % GROUP) == c, 1.0, 0.0).astype(BF16)
     turned = [
@@ -72,13 +73,6 @@
         )
         for p in range(PCOL)
     ]
-    bpad[...] = jnp.zeros_like(bpad)
-    bpad[:, SEARCH : SEARCH + W] = b.astype(F32)
-    wgt[...] = jnp.zeros_like(wgt)
-    for j in range(JN):
-        for p in range(PCOL):
-            at = PATCH * p + GROUP * j
-            wgt[pl.ds(j * PCOL * EXT + p * EXT, EXT), pl.ds(64 * p, 64)] = bpad[:, at : at + 64].astype(BF16)
     lane = iota((PATCH, PATCH), 1)
     tiles = PCOL * EXT // PATCH
     for u in range(SPAN):
@@ -95,6 +89,26 @@
             val = parts[tile].astype(BF16)
             for j in range(JN):
                 lhs[pl.ds(u * GROUP, GROUP), pl.ds((j * tiles + tile) * PATCH, PATCH)] = val[GROUP * j : GROUP * (j + 1)]
+    xr, xc = iota((W, 64 * PCOL), 0), iota((W, 64 * PCOL), 1)
+    af = a.astype(F32)
+    own = jnp.sum(af * af, axis=0, keepdims=True)
+    own_hi = own.astype(BF16)
+    own_lo = (own - own_hi.astype(F32)).astype(BF16)
+    same = jnp.where(xr // PATCH == xc // 64, 1.0, 0.0).astype(BF16)
+    own8 = jnp.concatenate([own_hi, own_lo, jnp.zeros((14, W), BF16)], axis=0)
+    own_sum = mm(own8, same)
+    energy_own = own_sum[0:1] + own_sum[1:2]
+    own_scale[...] = jnp.broadcast_to(lax.rsqrt(jnp.maximum(energy_own, FLOOR)), own_scale.shape)
+
+
+def correlate(b, own_scale, flags_ref, out_ref, lhs, bpad, wgt, prod):
+    bpad[...] = jnp.zeros_like(bpad)
+    bpad[:, SEARCH : SEARCH + W] = b.astype(F32)
+    wgt[...] = jnp.zeros_like(wgt)
+    for j in range(JN):
+        for p in range(PCOL):
+            at = PATCH * p + GROUP * j
+            wgt[pl.ds(j * PCOL * EXT + p * EXT, EXT), pl.ds(64 * p, 64)] = bpad[:, at : at + 64].astype(BF16)
     prod[...] = mm(lhs[...], wgt[...])
     rows = []
     pieces = []
@@ -121,16 +135,7 @@
     start = (xc // 64) * PATCH + (xc % 64) - SEARCH
     horiz = jnp.where((xr >= start) & (xr < start + PATCH), 1.0, 0.0).astype(BF16)
     energy_next = (mm(col_hi, horiz) + mm(col_lo, horiz))[:SPAN]
-    af = a.astype(F32)
-    own = jnp.sum(af * af, axis=0, keepdims=True)
-    own_hi = own.astype(BF16)
-    own_lo = (own - own_hi.astype(F32)).astype(BF16)
-    same = jnp.where(xr // PATCH == xc // 64, 1.0, 0.0).astype(BF16)
-    own8 = jnp.concatenate([own_hi, own_lo, jnp.zeros((14, W), BF16)], axis=0)
-    own_sum = mm(own8, same)
-    energy_own = own_sum[0:1] + own_sum[1:2]
-    floor_value = FLOOR_SHARE * PATCH * PATCH
-    scale = lax.rsqrt(jnp.maximum(energy_own, floor_value)) * lax.rsqrt(jnp.maximum(energy_next, floor_value))
+    scale = own_scale[0:1] * lax.rsqrt(jnp.maximum(energy_next, FLOOR))
     score = numer * scale
     score = jnp.concatenate([score, jnp.zeros((40 - SPAN, 64 * PCOL), F32)], axis=0)
     ur, lane = iota((40, PATCH), 0), iota((40, PATCH), 1)
@@ -157,57 +162,165 @@
 
 VMEM = pl.BlockSpec(memory_space=pltpu.VMEM)
 SMEM = pl.BlockSpec(memory_space=pltpu.SMEM)
-HALO = 32
-
-
-def normalize_body(low_ref, mid_ref, high_ref, tissue_ref, out_ref):
-    low, high = low_ref[...], high_ref[...]
-    x = jnp.concatenate([low[SEARCH - BOX : HALO], mid_ref[...], high[: HALO - (SEARCH - BOX)]], axis=0)
-    tissue = jnp.concatenate(
-        [low[HALO:].astype(F32), tissue_ref[...].astype(F32), high[HALO:].astype(F32)], axis=0
-    )
-    out_ref[...] = normalized(x, tissue, band())
-
-
-def correlate_body(own_ref, next_ref, flags_ref, out_ref, *scratch):
-    correlate(own_ref[SEARCH : SEARCH + PATCH], next_ref[...], flags_ref, out_ref, *scratch)
-
-
-def halo(image, tissue, top):
-    if top:
-        return jnp.concatenate([image[:HALO], tissue[:SEARCH].astype(BF16)], axis=0)
-    return jnp.concatenate([image[-HALO:], tissue[-SEARCH:].astype(BF16)], axis=0)
+RIM = 2 * BOX
+INNER = PATCH - 2 * BOX
+SLAB = RIM + 2 * BOX
+FAR_SLAB = 40
+FAR = 7
+PARAMS = pltpu.CompilerParams(vmem_limit_bytes=48 << 20)
+LONG = pl.CostEstimate(flops=1 << 33, bytes_accessed=1 << 20, transcendentals=0)
+SHORT = pl.CostEstimate(flops=1, bytes_accessed=1, transcendentals=0)
+
+
+def prepare_body(image_hbm, tissue_hbm, core_ref, first_ref, second_ref, first_far_ref, second_far_ref, image, tissue, sems):
+    copies = [
+        pltpu.make_async_copy(image_hbm, image, sems.at[0]),
+        pltpu.make_async_copy(tissue_hbm, tissue, sems.at[1]),
+    ]
+    for copy in copies:
+        copy.start()
+    for copy in copies:
+        copy.wait()
+    x = image[...].astype(F32)
+    marks = tissue[...].astype(F32)
+    inner = normalized(x, marks[BOX : PATCH - BOX], band())
+    top, bottom = x[:RIM], x[PATCH - RIM :]
+    top_marks, bottom_marks = marks[:BOX], marks[PATCH - BOX :]
+    core_ref[:INNER] = inner
+    core_ref[INNER:] = jnp.concatenate([top, bottom, top_marks, bottom_marks], axis=0).astype(BF16)
+    inner = inner.astype(F32)
+    upper = jnp.concatenate([inner[:BOX], top, top_marks], axis=0).astype(BF16)
+    lower = jnp.concatenate([inner[INNER - BOX :], bottom, bottom_marks], axis=0).astype(BF16)
+    even = lax.axis_index("xy") % 2 == 0
+
+    @pl.when(even)
+    def _():
+        first_ref[...] = upper
+        second_ref[...] = lower
+        first_far_ref[:SLAB] = upper
+        second_far_ref[:SLAB] = lower
+
+    @pl.when(jnp.logical_not(even))
+    def _():
+        first_ref[...] = lower
+        second_ref[...] = upper
+        first_far_ref[:SLAB] = lower
+        second_far_ref[:SLAB] = upper
+
+
+def completed(core, first, second):
+    keep = jnp.where(lax.axis_index("xy") % 2 == 0, 1.0, 0.0).astype(F32)
+    core, first, second = core.astype(F32), first.astype(F32), second.astype(F32)
+    low = first * keep + second * (1.0 - keep)
+    high = second * keep + first * (1.0 - keep)
+    edges = core[INNER:]
+    g = band()
+    x = jnp.concatenate([low[BOX : BOX + RIM], edges[:RIM]], axis=0)
+    tissue = jnp.concatenate([low[BOX + RIM :], edges[2 * RIM : 2 * RIM + BOX]], axis=0)
+    above = normalized(x, tissue, g).astype(F32)
+    x = jnp.concatenate([edges[RIM : 2 * RIM], high[BOX : BOX + RIM]], axis=0)
+    tissue = jnp.concatenate([edges[2 * RIM + BOX :], high[BOX + RIM :]], axis=0)
+    below = normalized(x, tissue, g).astype(F32)
+    return jnp.concatenate([low[:BOX], above, core[:INNER], below, high[:BOX]], axis=0)
+
+
+def complete_body(core_ref, first_ref, second_ref, out_ref):
+    out_ref[...] = completed(core_ref[...], first_ref[...], second_ref[...]).astype(BF16)
+
+
+def shifted_body(own_ref, lhs_ref, own_scale_ref):
+    shifted(own_ref[SEARCH : SEARCH + PATCH], lhs_ref, own_scale_ref)
+
+
+def is_far():
+    return lax.axis_index("sec") == FAR
+
+
+def far_body(core_ref, first_ref, second_ref, own_scale_ref, out_ref):
+    @pl.when(is_far())
+    def _():
+        out_ref[...] = completed(core_ref[...], first_ref[:SLAB], second_ref[:SLAB]).astype(BF16)
+
+
+def correlate_body(next_ref, far_ref, lhs_ref, own_scale_ref, flags_ref, out_ref, *scratch):
+    b = jnp.where(is_far(), far_ref[...].astype(F32), next_ref[...].astype(F32)).astype(BF16)
+    correlate(b, own_scale_ref[...], flags_ref, out_ref, lhs_ref, *scratch)
+
+
+def odd_partner(i):
+    return i - 1 if i % 2 == 0 else i + 1
+
+
+def even_partner(i):
+    return i + 1 if i % 2 == 0 else i - 1
+
+
+def call(body, out_shape, operands, in_specs=None, scratch=(), cost=None):
+    several = isinstance(out_shape, tuple)
+    return pl.pallas_call(
+        body,
+        out_shape=out_shape,
+        in_specs=in_specs or [VMEM] * len(operands),
+        out_specs=(VMEM,) * len(out_shape) if several else VMEM,
+        scratch_shapes=scratch,
+        compiler_params=PARAMS,
+        cost_estimate=cost,
+    )(*operands)
 
 
 def shards(image, mask, flags):
     image, mask, flags = image[0], mask[0], flags[0, 0]
-    count = lax.axis_size("xy")
-    forward = [(i, i + 1) for i in range(count - 1)]
-    backward = [(b, a) for a, b in forward]
-    low = lax.ppermute(halo(image, mask, False), "xy", forward)
-    high = lax.ppermute(halo(image, mask, True), "xy", backward)
-    own = pl.pallas_call(
-        normalize_body,
-        out_shape=jax.ShapeDtypeStruct((EXT, W), BF16),
-        in_specs=[VMEM] * 4,
-        out_specs=VMEM,
-        compiler_params=pltpu.CompilerParams(vmem_limit_bytes=48 << 20),
-    )(low, image, high, mask)
-    sections = lax.axis_size("sec")
-    following = lax.ppermute(own, "sec", [(s + 1, s) for s in range(sections - 1)])
-    scores = pl.pallas_call(
+    strips, sections = lax.axis_size("xy"), lax.axis_size("sec")
+    odd = [(i, odd_partner(i)) for i in range(strips) if 0 <= odd_partner(i) < strips]
+    even = [(i, even_partner(i)) for i in range(strips)]
+
+    def rows(count):
+        return jax.ShapeDtypeStruct((count, W), BF16)
+
+    core, first, second, first_far, second_far = call(
+        prepare_body,
+        (rows(PATCH + 2 * RIM), rows(SLAB), rows(SLAB), rows(FAR_SLAB), rows(FAR_SLAB)),
+        (image, mask),
+        in_specs=[pl.BlockSpec(memory_space=pl.ANY)] * 2,
+        scratch=[
+            pltpu.VMEM((PATCH, W), BF16),
+            pltpu.VMEM((PATCH, W), jnp.int32),
+            pltpu.SemaphoreType.DMA((2,)),
+        ],
+    )
+
+    def from_far(block, pairs):
+        route = [((FAR + 1) * strips + a, FAR * strips + b) for a, b in pairs]
+        return lax.ppermute(block, ("sec", "xy"), route)
+
+    core_far = from_far(core, [(i, i) for i in range(strips)])
+    first_far = from_far(first_far, odd)
+    second_far = from_far(second_far, even)
+    first = lax.ppermute(first, "xy", odd)
+    second = lax.ppermute(second, "xy", even)
+    own = call(complete_body, rows(EXT), (core, first, second), cost=SHORT)
+    following = lax.ppermute(own, "sec", [(s + 1, s) for s in range(sections - 1) if s != FAR])
+    lhs, own_scale = call(
+        shifted_body,
+        (
+            jax.ShapeDtypeStruct((SPAN * GROUP, JN * PCOL * EXT), BF16),
+            jax.ShapeDtypeStruct((8, 64 * PCOL), F32),
+        ),
+        (own,),
+        cost=SHORT,
+    )
+    far = call(far_body, rows(EXT), (core_far, first_far, second_far, own_scale), cost=LONG)
+    scores = call(
         correlate_body,
-        out_shape=jax.ShapeDtypeStruct((PCOL, SPAN * SPAN), F32),
-        in_specs=[VMEM, VMEM, SMEM],
-        out_specs=VMEM,
-        scratch_shapes=[
+        jax.ShapeDtypeStruct((PCOL, SPAN * SPAN), F32),
+        (following, far, lhs, own_scale, flags),
+        in_specs=[VMEM] * 4 + [SMEM],
+        scratch=[
             pltpu.VMEM((EXT, W + PATCH), F32),
             pltpu.VMEM((JN * PCOL * EXT, 64 * PCOL), BF16),
-            pltpu.VMEM((SPAN * GROUP, JN * PCOL * EXT), BF16),
             pltpu.VMEM((SPAN * GROUP, 64 * PCOL), F32),
         ],
-        compiler_params=pltpu.CompilerParams(vmem_limit_bytes=48 << 20),
-    )(own, following, flags)
+    )
     return scores[None, None]
 
 

time: 41.4 us -> 33 us (0.80)
  the two profiles are of different devices: /device:TPU:127 before, /device:TPU:481 now
where the time goes in v2:
time: 33 us; the launch traced here: 32.7 us
  starting transfers between devices  21 us (64%)
  Pallas kernels  6.33 us (19%)
  waiting for transfers between devices  2.73 us (8%)
  local copies, waits for them, and re-layouts  2.47 us (7%)
    ppermute x1, starting transfers between devices, shards(): lax.ppermute(own, 'sec', [(s + 1, s) for s in range(sections - 1) if s !=...  12.3 us
    pallas_call x5, Pallas kernels, call(): pl.pallas_call(body, out_shape=out_shape, in_specs=in_specs or [VMEM] * l...  6.33 us
    ppermute x1, starting transfers between devices, shards(): first = lax.ppermute(first, 'xy', odd)  4.84 us
    ppermute x1, waiting for transfers between devices, shards(): second = lax.ppermute(second, 'xy', even)  2.72 us
    unnamed x6, local copies, waits for them, and re-layouts  2.47 us
    ppermute x3, starting transfers between devices, from_far(): return lax.ppermute(block, ('sec', 'xy'), route)  2 us
    ppermute x1, starting transfers between devices, shards(): second = lax.ppermute(second, 'xy', even)  1.92 us
  transfers between devices with their start and end apart: 6, of which 1 were waited for; matrix products, arithmetic and copies ran while one was open for 0% of the time, Pallas kernels for 6%

profile of v2, /device:TPU:481, one launch (start us, length us, event | category | flops | bytes accessed | tf_op | source)
XLA Modules:
  0.0 32.7 jit_solution(9286579753283839946)
XLA Ops:
  0.0 0.0 copy-start
  0.0 0.9 %copy-done = s32[1,128,512]{2,1,0:T(8,128)S(1)} copy-done((s32[1,128,512]{2,1,0:T(8,128)S(1)}, s32[1,128,512]{2,1,0:T(8,128)}, u32[]{:S(2)}) %copy-start) | copy-done | bytes 262168
  1.0 0.0 copy-start.1
  1.0 0.9 %copy-done.1 = bf16[1,128,512]{2,1,0:T(8,128)(2,1)S(1)} copy-done((bf16[1,128,512]{2,1,0:T(8,128)(2,1)S(1)}, bf16[1,128,512]{2,1,0:T(8,128)(2,1)}, u32[]{:S(2)}) %copy-start.1) | copy-done | bytes 131096
  1.9 0.7 %shard_map.37 = (bf16[160,512]{1,0:T(8,128)(2,1)S(1)}, bf16[32,512]{1,0:T(8,128)(2,1)S(1)}, bf16[32,512]{1,0:T(8,128)(2,1)S(1)}, bf16[40,512]{1,0:T(8,128)(2,1)S(1)}, bf16[40,512]{1,0:T(8,128)(2,1)S(1)}) custom-call(bf16[128,512]{1,0:T(8,128)(2,1)S(1)} %bitcast.5, s32[128,512]{1,0:T(8,128)S(1)} %bitcast.4), custom_call_target="tpu_custom_call" | custom-call | tf_op jit(solution)/shard_map/pallas_call | solution.py:260
  2.6 0.7 %collective-permute-start.3 = (bf16[160,512]{1,0:T(8,128)(2,1)S(1)}, bf16[160,512]{1,0:T(8,128)(2,1)S(1)}, u32[]{:S(2)}, u32[]{:S(2)}) collective-permute-start(bf16[160,512]{1,0:T(8,128)(2,1)S(1)} %get-tuple-element.12.core_ref), channel_id=1, source_target_pairs={{256,224},{257,225},{258,226},{259,227},{260,228},{261,229},{262,2... | collective-permute-start | bytes 491528 | tf_op jit(solution)/shard_map/ppermute | solution.py:294
  3.3 0.7 %collective-permute-start.4 = (bf16[40,512]{1,0:T(8,128)(2,1)S(1)}, bf16[40,512]{1,0:T(8,128)(2,1)S(1)}, u32[]{:S(2)}, u32[]{:S(2)}) collective-permute-start(bf16[40,512]{1,0:T(8,128)(2,1)S(1)} %get-tuple-element.15), channel_id=1, source_target_pairs={{257,226},{258,225},{259,228},{260,227},{261,230},{262,229},{263,2... | collective-permute-start | bytes 122888 | tf_op jit(solution)/shard_map/ppermute | solution.py:294
  4.0 0.7 %collective-permute-start.5 = (bf16[40,512]{1,0:T(8,128)(2,1)S(1)}, bf16[40,512]{1,0:T(8,128)(2,1)S(1)}, u32[]{:S(2)}, u32[]{:S(2)}) collective-permute-start(bf16[40,512]{1,0:T(8,128)(2,1)S(1)} %get-tuple-element.16), channel_id=1, source_target_pairs={{256,225},{257,224},{258,227},{259,226},{260,229},{261,228},{262,2... | collective-permute-start | bytes 122888 | tf_op jit(solution)/shard_map/ppermute | solution.py:294
  4.6 4.8 %collective-permute-start = (bf16[32,512]{1,0:T(8,128)(2,1)S(1)}, bf16[32,512]{1,0:T(8,128)(2,1)S(1)}, u32[]{:S(2)}, u32[]{:S(2)}) collective-permute-start(bf16[32,512]{1,0:T(8,128)(2,1)S(1)} %get-tuple-element.13), channel_id=1, source_target_pairs={{1,2},{2,1},{3,4},{4,3},{5,6},{6,5},{7,8},{8,7},{9,10},{10,9},{11,... | collective-permute-start | bytes 98312 | tf_op jit(solution)/shard_map/ppermute | solution.py:299
  9.5 1.9 %collective-permute-start.1 = (bf16[32,512]{1,0:T(8,128)(2,1)S(1)}, bf16[32,512]{1,0:T(8,128)(2,1)S(1)}, u32[]{:S(2)}, u32[]{:S(2)}) collective-permute-start(bf16[32,512]{1,0:T(8,128)(2,1)S(1)} %get-tuple-element.14), channel_id=1, source_target_pairs={{0,1},{1,0},{2,3},{3,2},{4,5},{5,4},{6,7},{7,6},{8,9},{9,8},{10,11... | collective-permute-start | bytes 98312 | tf_op jit(solution)/shard_map/ppermute | solution.py:300
  11.4 0.0 collective-permute-done.first_ref
  11.4 2.7 %collective-permute-done.1.second_ref = bf16[32,512]{1,0:T(8,128)(2,1)S(1)} collective-permute-done((bf16[32,512]{1,0:T(8,128)(2,1)S(1)}, bf16[32,512]{1,0:T(8,128)(2,1)S(1)}, u32[]{:S(2)}, u32[]{:S(2)}) %collective-permute-start.1) | collective-permute-done | bytes 32800 | tf_op jit(solution)/shard_map/ppermute | solution.py:300
  14.1 0.5 %shard_map.38.own_ref = bf16[160,512]{1,0:T(8,128)(2,1)S(1)} custom-call(bf16[160,512]{1,0:T(8,128)(2,1)S(1)} %get-tuple-element.12.core_ref, bf16[32,512]{1,0:T(8,128)(2,1)S(1)} %collective-permute-done.first_ref, bf16[32,512]{1,0:T(8,128)(2,1)S(1)} %collective-permute-done.1.second_ref), custom_call_target="tpu_custom_call" | custom-call | flops 1 | bytes 1 | tf_op jit(solution)/shard_map/pallas_call | solution.py:260
  14.6 12.3 %collective-permute-start.2 = (bf16[160,512]{1,0:T(8,128)(2,1)S(1)}, bf16[160,512]{1,0:T(8,128)(2,1)S(1)}, u32[]{:S(2)}, u32[]{:S(2)}) collective-permute-start(bf16[160,512]{1,0:T(8,128)(2,1)S(1)} %shard_map.38.own_ref), channel_id=1, source_target_pairs={{32,0},{64,32},{96,64},{128,96},{160,128},{192,160},{224,192},{288... | collective-permute-start | bytes 491528 | tf_op jit(solution)/shard_map/ppermute | solution.py:302
  26.9 1.5 %shard_map.39 = (bf16[1056,2560]{1,0:T(8,128)(2,1)S(1)}, f32[8,256]{1,0:T(8,128)S(1)}) custom-call(bf16[160,512]{1,0:T(8,128)(2,1)S(1)} %shard_map.38.own_ref), custom_call_target="tpu_custom_call" | custom-call | flops 1 | bytes 1 | tf_op jit(solution)/shard_map/pallas_call | solution.py:260
  28.5 0.0 collective-permute-done.4.first_ref
  28.5 0.0 collective-permute-done.5.second_ref
  28.5 0.0 collective-permute-done.3.core_ref
  28.5 0.0 copy-start.2
  28.5 0.0 collective-permute-done.2.next_ref
  28.5 0.6 %copy-done.2 = s32[1,1,4]{2,1,0:T(1,128)S(1)} copy-done((s32[1,1,4]{2,1,0:T(1,128)S(1)}, s32[1,1,4]{2,1,0:T(1,128)}, u32[]{:S(2)}) %copy-start.2) | copy-done | bytes 40
  29.1 3.6 %shard_map.41 = f32[4,1089]{1,0:T(4,128)} custom-call(bf16[160,512]{1,0:T(8,128)(2,1)S(1)} %collective-permute-done.2.next_ref, bf16[160,512]{1,0:T(8,128)(2,1)S(1)} %shard_map.40.far_ref, bf16[1056,2560]{1,0:T(8,128)(2,1)S(1)} %get-tuple-element.18.lhs_ref, f32[8,256]{1,0:T(8,128)S(1)} %get-tuple-element.17.own_scale_ref, s32[4]{0:T(128)S(1)} %bitcast.6), custom_call_target="tpu_custom_call" | custom-call | tf_op jit(solution)/shard_map/pallas_call | solution.py:260
  (1 shorter events, 0.0 us)
Async XLA Ops:
  0.0 0.9 %copy-start = (s32[1,128,512]{2,1,0:T(8,128)S(1)}, s32[1,128,512]{2,1,0:T(8,128)}, u32[]{:S(2)}) copy-start(s32[1,128,512]{2,1,0:T(8,128)} %param.4) | copy-start | bytes 786436
  1.0 0.9 %copy-start.1 = (bf16[1,128,512]{2,1,0:T(8,128)(2,1)S(1)}, bf16[1,128,512]{2,1,0:T(8,128)(2,1)}, u32[]{:S(2)}) copy-start(bf16[1,128,512]{2,1,0:T(8,128)(2,1)} %param.3) | copy-start | bytes 393220
  2.6 25.9 %collective-permute-start.3 = (bf16[160,512]{1,0:T(8,128)(2,1)S(1)}, bf16[160,512]{1,0:T(8,128)(2,1)S(1)}, u32[]{:S(2)}, u32[]{:S(2)}) collective-permute-start(bf16[160,512]{1,0:T(8,128)(2,1)S(1)} %get-tuple-element.12.core_ref), channel_id=1, source_target_pairs={{256,224},{257,225},{258,226},{259,227},{260,228},{261,229},{262,2... | collective-permute-start | bytes 491528 | tf_op jit(solution)/shard_map/ppermute | solution.py:294
  3.3 25.2 %collective-permute-start.4 = (bf16[40,512]{1,0:T(8,128)(2,1)S(1)}, bf16[40,512]{1,0:T(8,128)(2,1)S(1)}, u32[]{:S(2)}, u32[]{:S(2)}) collective-permute-start(bf16[40,512]{1,0:T(8,128)(2,1)S(1)} %get-tuple-element.15), channel_id=1, source_target_pairs={{257,226},{258,225},{259,228},{260,227},{261,230},{262,229},{263,2... | collective-permute-start | bytes 122888 | tf_op jit(solution)/shard_map/ppermute | solution.py:294
  4.0 24.5 %collective-permute-start.5 = (bf16[40,512]{1,0:T(8,128)(2,1)S(1)}, bf16[40,512]{1,0:T(8,128)(2,1)S(1)}, u32[]{:S(2)}, u32[]{:S(2)}) collective-permute-start(bf16[40,512]{1,0:T(8,128)(2,1)S(1)} %get-tuple-element.16), channel_id=1, source_target_pairs={{256,225},{257,224},{258,227},{259,226},{260,229},{261,228},{262,2... | collective-permute-start | bytes 122888 | tf_op jit(solution)/shard_map/ppermute | solution.py:294
  4.6 6.8 %collective-permute-start = (bf16[32,512]{1,0:T(8,128)(2,1)S(1)}, bf16[32,512]{1,0:T(8,128)(2,1)S(1)}, u32[]{:S(2)}, u32[]{:S(2)}) collective-permute-start(bf16[32,512]{1,0:T(8,128)(2,1)S(1)} %get-tuple-element.13), channel_id=1, source_target_pairs={{1,2},{2,1},{3,4},{4,3},{5,6},{6,5},{7,8},{8,7},{9,10},{10,9},{11,... | collective-permute-start | bytes 98312 | tf_op jit(solution)/shard_map/ppermute | solution.py:299
  9.5 4.7 %collective-permute-start.1 = (bf16[32,512]{1,0:T(8,128)(2,1)S(1)}, bf16[32,512]{1,0:T(8,128)(2,1)S(1)}, u32[]{:S(2)}, u32[]{:S(2)}) collective-permute-start(bf16[32,512]{1,0:T(8,128)(2,1)S(1)} %get-tuple-element.14), channel_id=1, source_target_pairs={{0,1},{1,0},{2,3},{3,2},{4,5},{5,4},{6,7},{7,6},{8,9},{9,8},{10,11... | collective-permute-start | bytes 98312 | tf_op jit(solution)/shard_map/ppermute | solution.py:300
  14.6 13.9 %collective-permute-start.2 = (bf16[160,512]{1,0:T(8,128)(2,1)S(1)}, bf16[160,512]{1,0:T(8,128)(2,1)S(1)}, u32[]{:S(2)}, u32[]{:S(2)}) collective-permute-start(bf16[160,512]{1,0:T(8,128)(2,1)S(1)} %shard_map.38.own_ref), channel_id=1, source_target_pairs={{32,0},{64,32},{96,64},{128,96},{160,128},{192,160},{224,192},{288... | collective-permute-start | bytes 491528 | tf_op jit(solution)/shard_map/ppermute | solution.py:302
  28.5 0.7 %copy-start.2 = (s32[1,1,4]{2,1,0:T(1,128)S(1)}, s32[1,1,4]{2,1,0:T(1,128)}, u32[]{:S(2)}) copy-start(s32[1,1,4]{2,1,0:T(1,128)} %param.5) | copy-start | bytes 52

commit v3 on v2

--- a/solution.py
+++ b/solution.py
@@ -64,7 +64,7 @@
     return (tissue * scaled).astype(BF16)
 
 
-def shifted(a, lhs, own_scale):
+def shifted(a, valid, lhs, own_scale):
     r, c = iota((PATCH, PATCH), 0), iota((PATCH, PATCH), 1)
     flip = jnp.where((r // GROUP) * GROUP + (GROUP - 1 - r % GROUP) == c, 1.0, 0.0).astype(BF16)
     turned = [
@@ -98,70 +98,71 @@
     own8 = jnp.concatenate([own_hi, own_lo, jnp.zeros((14, W), BF16)], axis=0)
     own_sum = mm(own8, same)
     energy_own = own_sum[0:1] + own_sum[1:2]
-    own_scale[...] = jnp.broadcast_to(lax.rsqrt(jnp.maximum(energy_own, FLOOR)), own_scale.shape)
-
-
-def correlate(b, own_scale, flags_ref, out_ref, lhs, bpad, wgt, prod):
-    bpad[...] = jnp.zeros_like(bpad)
-    bpad[:, SEARCH : SEARCH + W] = b.astype(F32)
-    wgt[...] = jnp.zeros_like(wgt)
-    for j in range(JN):
-        for p in range(PCOL):
-            at = PATCH * p + GROUP * j
-            wgt[pl.ds(j * PCOL * EXT + p * EXT, EXT), pl.ds(64 * p, 64)] = bpad[:, at : at + 64].astype(BF16)
+    own_scale[...] = valid * lax.rsqrt(jnp.maximum(energy_own, FLOOR))
+
+
+def correlate(b, own_scale, out_ref, lhs, wide, wgt, prod):
+    wide[:, :PATCH] = jnp.zeros((EXT, PATCH), F32)
+    wide[:, W:] = jnp.zeros((EXT, PATCH), F32)
+    wide[:, SEARCH : SEARCH + W] = b
+    lane = iota((EXT, PATCH), 1)
+    for p in range(PCOL):
+        h, q = divmod(p, 2)
+        one, two = wide[:, PATCH * p : PATCH * (p + 1)], wide[:, PATCH * (p + 1) : PATCH * (p + 2)]
+        for j in range(JN):
+            turn = (64 * q - GROUP * j) % PATCH
+            piece = pltpu.roll(one, turn, 1) if turn else one
+            if j == JN - 1:
+                piece = jnp.where(lane < 64 * q + GROUP, piece, pltpu.roll(two, turn, 1) if turn else two)
+            rows = pl.ds((j * PCOL + p) * EXT, EXT)
+            keep = lane < 64 if q == 0 else lane >= 64
+            wgt[rows, pl.ds(PATCH * h, PATCH)] = jnp.where(keep, piece, 0.0).astype(BF16)
+            wgt[rows, pl.ds(PATCH * (1 - h), PATCH)] = jnp.zeros((EXT, PATCH), BF16)
     prod[...] = mm(lhs[...], wgt[...])
-    rows = []
-    pieces = []
+    sq = wide[...] * wide[...]
+    sq_hi = sq.astype(BF16)
+    sq_lo = (sq - sq_hi.astype(F32)).astype(BF16)
+    r, c = iota((40, EXT), 0), iota((40, EXT), 1)
+    vert = jnp.where((c >= r) & (c < r + PATCH), 1.0, 0.0).astype(BF16)
+    col = mm(vert, sq_hi) + mm(vert, sq_lo)
+    col_hi = col.astype(BF16)
+    col_lo = (col - col_hi.astype(F32)).astype(BF16)
+    parts = jnp.concatenate([col_hi, col_lo], axis=0)
+    r, c = iota((2 * PATCH, PATCH), 0), iota((2 * PATCH, PATCH), 1) % 64
+    horiz = jnp.where((r >= c) & (r < c + PATCH), 1.0, 0.0).astype(BF16)
+    sums = [mm(parts[:, PATCH * p : PATCH * (p + 2)], horiz) for p in range(PCOL)]
+    left = iota((40, PATCH), 1) < 64
+    energies = [jnp.where(left, sums[2 * h][:40] + sums[2 * h][40:], sums[2 * h + 1][:40] + sums[2 * h + 1][40:]) for h in range(2)]
+    ur, lane = iota((40, PATCH), 0), iota((40, PATCH), 1)
     for h in range(2):
         block = prod[:, pl.ds(PATCH * h, PATCH)].reshape(SPAN, JN, 8, PATCH)
         total = None
         for q in range(GROUP // 8):
-            part = block[:, q].reshape(SPAN * 8, PATCH)
-            part = part.reshape(SPAN, 8, PATCH)
+            part = block[:, q]
             moved = pltpu.roll(part, PATCH - (GROUP - 1) + 8 * q, 2, stride=1, stride_axis=1)
             total = moved if total is None else total + moved
-        pieces.append(jnp.sum(total, axis=1))
-    numer = jnp.concatenate(pieces, axis=1)
-    bf = b.astype(F32)
-    sq = bf * bf
-    sq_hi = sq.astype(BF16)
-    sq_lo = (sq - sq_hi.astype(F32)).astype(BF16)
-    ur, uc = iota((40, EXT), 0), iota((40, EXT), 1)
-    vert = jnp.where((uc >= ur) & (uc < ur + PATCH), 1.0, 0.0).astype(BF16)
-    col = mm(vert, sq_hi) + mm(vert, sq_lo)
-    col_hi = col.astype(BF16)
-    col_lo = (col - col_hi.astype(F32)).astype(BF16)
-    xr, xc = iota((W, 64 * PCOL), 0), iota((W, 64 * PCOL), 1)
-    start = (xc // 64) * PATCH + (xc % 64) - SEARCH
-    horiz = jnp.where((xr >= start) & (xr < start + PATCH), 1.0, 0.0).astype(BF16)
-    energy_next = (mm(col_hi, horiz) + mm(col_lo, horiz))[:SPAN]
-    scale = own_scale[0:1] * lax.rsqrt(jnp.maximum(energy_next, FLOOR))
-    score = numer * scale
-    score = jnp.concatenate([score, jnp.zeros((40 - SPAN, 64 * PCOL), F32)], axis=0)
-    ur, lane = iota((40, PATCH), 0), iota((40, PATCH), 1)
-    for h in range(2):
-        half = score[:, PATCH * h : PATCH * (h + 1)]
-        for s in range(2):
-            p = 2 * h + s
-            flag = flags_ref[p].astype(F32)
-            lines = []
-            for k in range(5):
-                rows8 = (half * flag)[8 * k : 8 * k + 8]
-                base = (8 * k - 64 * s) % PATCH
-                rows8 = pltpu.roll(rows8, base, 1) if base else rows8
-                rows8 = pltpu.roll(rows8, 0, 1, stride=16, stride_axis=0)
-                lines.append(pltpu.roll(rows8, 0, 1, stride=17, stride_axis=0))
-            moved = jnp.concatenate(lines, axis=0)
+        numer = jnp.sum(total, axis=1)
+        numer = jnp.concatenate([numer, jnp.zeros((40 - SPAN, PATCH), F32)], axis=0)
+        scale = own_scale[0:1, PATCH * h : PATCH * (h + 1)] * lax.rsqrt(jnp.maximum(energies[h], FLOOR))
+        score = numer * scale
+        lines = []
+        for k in range(5):
+            line = score[8 * k : 8 * k + 8]
+            line = pltpu.roll(line, 8 * k, 1) if k else line
+            line = pltpu.roll(line, 0, 1, stride=16, stride_axis=0)
+            lines.append(pltpu.roll(line, 0, 1, stride=17, stride_axis=0))
+        both = jnp.concatenate(lines, axis=0)
+        for q, moved in enumerate((both, pltpu.roll(both, 64, 1))):
+            p = 2 * h + q
             for t in range(9):
                 at = t * PATCH + lane
                 pick = (at >= SPAN * ur) & (at < SPAN * ur + SPAN)
                 line = jnp.sum(jnp.where(pick, moved, 0.0), axis=0, keepdims=True)
-                wide = min(PATCH, SPAN * SPAN - t * PATCH)
-                out_ref[p : p + 1, t * PATCH : t * PATCH + wide] = line[:, :wide]
+                count = min(PATCH, SPAN * SPAN - t * PATCH)
+                out_ref[p : p + 1, t * PATCH : t * PATCH + count] = line[:, :count]
 
 
 VMEM = pl.BlockSpec(memory_space=pltpu.VMEM)
-SMEM = pl.BlockSpec(memory_space=pltpu.SMEM)
 RIM = 2 * BOX
 INNER = PATCH - 2 * BOX
 SLAB = RIM + 2 * BOX
@@ -172,10 +173,14 @@
 SHORT = pl.CostEstimate(flops=1, bytes_accessed=1, transcendentals=0)
 
 
-def prepare_body(image_hbm, tissue_hbm, core_ref, first_ref, second_ref, first_far_ref, second_far_ref, image, tissue, sems):
+def prepare_body(
+    image_hbm, tissue_hbm, flags_hbm, core_ref, first_ref, second_ref, first_far_ref, second_far_ref, valid_ref,
+    image, tissue, flags, sems,
+):
     copies = [
         pltpu.make_async_copy(image_hbm, image, sems.at[0]),
         pltpu.make_async_copy(tissue_hbm, tissue, sems.at[1]),
+        pltpu.make_async_copy(flags_hbm, flags, sems.at[2]),
     ]
     for copy in copies:
         copy.start()
@@ -191,6 +196,11 @@
     inner = inner.astype(F32)
     upper = jnp.concatenate([inner[:BOX], top, top_marks], axis=0).astype(BF16)
     lower = jnp.concatenate([inner[INNER - BOX :], bottom, bottom_marks], axis=0).astype(BF16)
+    patch = iota((8, 64 * PCOL), 1) // 64
+    valid = jnp.zeros((8, 64 * PCOL), jnp.int32)
+    for p in range(PCOL):
+        valid = jnp.where(patch == p, flags[p], valid)
+    valid_ref[...] = valid.astype(F32)
     even = lax.axis_index("xy") % 2 == 0
 
     @pl.when(even)
@@ -228,8 +238,8 @@
     out_ref[...] = completed(core_ref[...], first_ref[...], second_ref[...]).astype(BF16)
 
 
-def shifted_body(own_ref, lhs_ref, own_scale_ref):
-    shifted(own_ref[SEARCH : SEARCH + PATCH], lhs_ref, own_scale_ref)
+def shifted_body(own_ref, valid_ref, lhs_ref, own_scale_ref):
+    shifted(own_ref[SEARCH : SEARCH + PATCH], valid_ref[...], lhs_ref, own_scale_ref)
 
 
 def is_far():
@@ -242,9 +252,9 @@
         out_ref[...] = completed(core_ref[...], first_ref[:SLAB], second_ref[:SLAB]).astype(BF16)
 
 
-def correlate_body(next_ref, far_ref, lhs_ref, own_scale_ref, flags_ref, out_ref, *scratch):
-    b = jnp.where(is_far(), far_ref[...].astype(F32), next_ref[...].astype(F32)).astype(BF16)
-    correlate(b, own_scale_ref[...], flags_ref, out_ref, lhs_ref, *scratch)
+def correlate_body(next_ref, far_ref, lhs_ref, own_scale_ref, out_ref, *scratch):
+    b = jnp.where(is_far(), far_ref[...].astype(F32), next_ref[...].astype(F32))
+    correlate(b, own_scale_ref[...], out_ref, lhs_ref, *scratch)
 
 
 def odd_partner(i):
@@ -277,15 +287,16 @@
     def rows(count):
         return jax.ShapeDtypeStruct((count, W), BF16)
 
-    core, first, second, first_far, second_far = call(
+    core, first, second, first_far, second_far, valid = call(
         prepare_body,
-        (rows(PATCH + 2 * RIM), rows(SLAB), rows(SLAB), rows(FAR_SLAB), rows(FAR_SLAB)),
-        (image, mask),
-        in_specs=[pl.BlockSpec(memory_space=pl.ANY)] * 2,
+        (rows(PATCH + 2 * RIM), rows(SLAB), rows(SLAB), rows(FAR_SLAB), rows(FAR_SLAB), jax.ShapeDtypeStruct((8, 64 * PCOL), F32)),
+        tuple(pltpu.with_memory_space_constraint(x, pltpu.HBM) for x in (image, mask, flags)),
+        in_specs=[pl.BlockSpec(memory_space=pltpu.HBM)] * 3,
         scratch=[
             pltpu.VMEM((PATCH, W), BF16),
             pltpu.VMEM((PATCH, W), jnp.int32),
-            pltpu.SemaphoreType.DMA((2,)),
+            pltpu.SMEM((PCOL,), jnp.int32),
+            pltpu.SemaphoreType.DMA((3,)),
         ],
     )
 
@@ -306,15 +317,14 @@
             jax.ShapeDtypeStruct((SPAN * GROUP, JN * PCOL * EXT), BF16),
             jax.ShapeDtypeStruct((8, 64 * PCOL), F32),
         ),
-        (own,),
+        (own, valid),
         cost=SHORT,
     )
     far = call(far_body, rows(EXT), (core_far, first_far, second_far, own_scale), cost=LONG)
     scores = call(
         correlate_body,
         jax.ShapeDtypeStruct((PCOL, SPAN * SPAN), F32),
-        (following, far, lhs, own_scale, flags),
-        in_specs=[VMEM] * 4 + [SMEM],
+        (following, far, lhs, own_scale),
         scratch=[
             pltpu.VMEM((EXT, W + PATCH), F32),
             pltpu.VMEM((JN * PCOL * EXT, 64 * PCOL), BF16),

time: 33 us -> 30.7 us (0.930)
  local copies, waits for them, and re-layouts: 2.47 us -> 0 us
    unnamed x6 -> x0, local copies, waits for them, and re-layouts: 2.47 us -> none
  transfers between devices with their start and end apart: 6 -> 6, of which waited for: 1 -> 1; matrix products, arithmetic and copies ran while one was open for 0% -> 0% of each run, Pallas kernels for 6% -> 7%
where the time goes in v3:
time: 30.7 us; the launch traced here: 30.5 us
  starting transfers between devices  21 us (68%)
  Pallas kernels  6.56 us (21%)
  waiting for transfers between devices  2.73 us (9%)
    ppermute x1, starting transfers between devices, shards(): lax.ppermute(own, 'sec', [(s + 1, s) for s in range(sections - 1) if s !=...  12.3 us
    pallas_call x5, Pallas kernels, call(): pl.pallas_call(body, out_shape=out_shape, in_specs=in_specs or [VMEM] * l...  6.56 us
    ppermute x1, starting transfers between devices, shards(): first = lax.ppermute(first, 'xy', odd)  4.84 us
    ppermute x1, waiting for transfers between devices, shards(): second = lax.ppermute(second, 'xy', even)  2.72 us
    ppermute x3, starting transfers between devices, from_far(): return lax.ppermute(block, ('sec', 'xy'), route)  2 us
    ppermute x1, starting transfers between devices, shards(): second = lax.ppermute(second, 'xy', even)  1.92 us
  transfers between devices with their start and end apart: 6, of which 1 were waited for; matrix products, arithmetic and copies ran while one was open for 0% of the time, Pallas kernels for 7%

profile of v3, /device:TPU:481, one launch (start us, length us, event | category | flops | bytes accessed | tf_op | source)
XLA Modules:
  0.0 30.5 jit_solution(13243780671059345102)
XLA Ops:
  0.0 1.6 %shard_map.37 = (bf16[160,512]{1,0:T(8,128)(2,1)S(1)}, bf16[32,512]{1,0:T(8,128)(2,1)S(1)}, bf16[32,512]{1,0:T(8,128)(2,1)S(1)}, bf16[40,512]{1,0:T(8,128)(2,1)S...) custom-call(bf16[128,512]{1,0:T(8,128)(2,1)} %bitcast.5, s32[128,512]{1,0:T(8,128)} %bitcast.4, s32[4]{0:T(128)} %bitcast.6), custom_call_target="tpu_custom_call" | custom-call | tf_op jit(solution)/shard_map/pallas_call | solution.py:270
  1.6 0.7 %collective-permute-start.3 = (bf16[160,512]{1,0:T(8,128)(2,1)S(1)}, bf16[160,512]{1,0:T(8,128)(2,1)S(1)}, u32[]{:S(2)}, u32[]{:S(2)}) collective-permute-start(bf16[160,512]{1,0:T(8,128)(2,1)S(1)} %get-tuple-element.13.core_ref), channel_id=1, source_target_pairs={{256,224},{257,225},{258,226},{259,227},{260,228},{261,229},{262,2... | collective-permute-start | bytes 491528 | tf_op jit(solution)/shard_map/ppermute | solution.py:305
  2.3 0.7 %collective-permute-start.4 = (bf16[40,512]{1,0:T(8,128)(2,1)S(1)}, bf16[40,512]{1,0:T(8,128)(2,1)S(1)}, u32[]{:S(2)}, u32[]{:S(2)}) collective-permute-start(bf16[40,512]{1,0:T(8,128)(2,1)S(1)} %get-tuple-element.16), channel_id=1, source_target_pairs={{257,226},{258,225},{259,228},{260,227},{261,230},{262,229},{263,2... | collective-permute-start | bytes 122888 | tf_op jit(solution)/shard_map/ppermute | solution.py:305
  3.0 0.7 %collective-permute-start.5 = (bf16[40,512]{1,0:T(8,128)(2,1)S(1)}, bf16[40,512]{1,0:T(8,128)(2,1)S(1)}, u32[]{:S(2)}, u32[]{:S(2)}) collective-permute-start(bf16[40,512]{1,0:T(8,128)(2,1)S(1)} %get-tuple-element.17), channel_id=1, source_target_pairs={{256,225},{257,224},{258,227},{259,226},{260,229},{261,228},{262,2... | collective-permute-start | bytes 122888 | tf_op jit(solution)/shard_map/ppermute | solution.py:305
  3.7 4.8 %collective-permute-start = (bf16[32,512]{1,0:T(8,128)(2,1)S(1)}, bf16[32,512]{1,0:T(8,128)(2,1)S(1)}, u32[]{:S(2)}, u32[]{:S(2)}) collective-permute-start(bf16[32,512]{1,0:T(8,128)(2,1)S(1)} %get-tuple-element.14), channel_id=1, source_target_pairs={{1,2},{2,1},{3,4},{4,3},{5,6},{6,5},{7,8},{8,7},{9,10},{10,9},{11,... | collective-permute-start | bytes 98312 | tf_op jit(solution)/shard_map/ppermute | solution.py:310
  8.5 1.9 %collective-permute-start.1 = (bf16[32,512]{1,0:T(8,128)(2,1)S(1)}, bf16[32,512]{1,0:T(8,128)(2,1)S(1)}, u32[]{:S(2)}, u32[]{:S(2)}) collective-permute-start(bf16[32,512]{1,0:T(8,128)(2,1)S(1)} %get-tuple-element.15), channel_id=1, source_target_pairs={{0,1},{1,0},{2,3},{3,2},{4,5},{5,4},{6,7},{7,6},{8,9},{9,8},{10,11... | collective-permute-start | bytes 98312 | tf_op jit(solution)/shard_map/ppermute | solution.py:311
  10.4 0.0 collective-permute-done.first_ref
  10.4 2.7 %collective-permute-done.1.second_ref = bf16[32,512]{1,0:T(8,128)(2,1)S(1)} collective-permute-done((bf16[32,512]{1,0:T(8,128)(2,1)S(1)}, bf16[32,512]{1,0:T(8,128)(2,1)S(1)}, u32[]{:S(2)}, u32[]{:S(2)}) %collective-permute-start.1) | collective-permute-done | bytes 32800 | tf_op jit(solution)/shard_map/ppermute | solution.py:311
  13.2 0.5 %shard_map.38.own_ref = bf16[160,512]{1,0:T(8,128)(2,1)S(1)} custom-call(bf16[160,512]{1,0:T(8,128)(2,1)S(1)} %get-tuple-element.13.core_ref, bf16[32,512]{1,0:T(8,128)(2,1)S(1)} %collective-permute-done.first_ref, bf16[32,512]{1,0:T(8,128)(2,1)S(1)} %collective-permute-done.1.second_ref), custom_call_target="tpu_custom_call" | custom-call | flops 1 | bytes 1 | tf_op jit(solution)/shard_map/pallas_call | solution.py:270
  13.7 12.3 %collective-permute-start.2 = (bf16[160,512]{1,0:T(8,128)(2,1)S(1)}, bf16[160,512]{1,0:T(8,128)(2,1)S(1)}, u32[]{:S(2)}, u32[]{:S(2)}) collective-permute-start(bf16[160,512]{1,0:T(8,128)(2,1)S(1)} %shard_map.38.own_ref), channel_id=1, source_target_pairs={{32,0},{64,32},{96,64},{128,96},{160,128},{192,160},{224,192},{288... | collective-permute-start | bytes 491528 | tf_op jit(solution)/shard_map/ppermute | solution.py:313
  25.9 1.5 %shard_map.39 = (bf16[1056,2560]{1,0:T(8,128)(2,1)S(1)}, f32[8,256]{1,0:T(8,128)S(1)}) custom-call(bf16[160,512]{1,0:T(8,128)(2,1)S(1)} %shard_map.38.own_ref, f32[8,256]{1,0:T(8,128)S(1)} %get-tuple-element.18.valid_ref), custom_call_target="tpu_custom_call" | custom-call | flops 1 | bytes 1 | tf_op jit(solution)/shard_map/pallas_call | solution.py:270
  27.5 0.0 collective-permute-done.4.first_ref
  27.5 0.0 collective-permute-done.5.second_ref
  27.5 0.0 collective-permute-done.3.core_ref
  27.5 0.0 collective-permute-done.2.next_ref
  27.5 2.9 %shard_map.41 = f32[4,1089]{1,0:T(4,128)} custom-call(bf16[160,512]{1,0:T(8,128)(2,1)S(1)} %collective-permute-done.2.next_ref, bf16[160,512]{1,0:T(8,128)(2,1)S(1)} %shard_map.40.far_ref, bf16[1056,2560]{1,0:T(8,128)(2,1)S(1)} %get-tuple-element.20.lhs_ref, f32[8,256]{1,0:T(8,128)S(1)} %get-tuple-element.19.own_scale_ref), custom_call_target="tpu_custom_call" | custom-call | tf_op jit(solution)/shard_map/pallas_call | solution.py:270
  (1 shorter events, 0.0 us)
Async XLA Ops:
  1.6 25.9 %collective-permute-start.3 = (bf16[160,512]{1,0:T(8,128)(2,1)S(1)}, bf16[160,512]{1,0:T(8,128)(2,1)S(1)}, u32[]{:S(2)}, u32[]{:S(2)}) collective-permute-start(bf16[160,512]{1,0:T(8,128)(2,1)S(1)} %get-tuple-element.13.core_ref), channel_id=1, source_target_pairs={{256,224},{257,225},{258,226},{259,227},{260,228},{261,229},{262,2... | collective-permute-start | bytes 491528 | tf_op jit(solution)/shard_map/ppermute | solution.py:305
  2.3 25.2 %collective-permute-start.4 = (bf16[40,512]{1,0:T(8,128)(2,1)S(1)}, bf16[40,512]{1,0:T(8,128)(2,1)S(1)}, u32[]{:S(2)}, u32[]{:S(2)}) collective-permute-start(bf16[40,512]{1,0:T(8,128)(2,1)S(1)} %get-tuple-element.16), channel_id=1, source_target_pairs={{257,226},{258,225},{259,228},{260,227},{261,230},{262,229},{263,2... | collective-permute-start | bytes 122888 | tf_op jit(solution)/shard_map/ppermute | solution.py:305
  3.0 24.5 %collective-permute-start.5 = (bf16[40,512]{1,0:T(8,128)(2,1)S(1)}, bf16[40,512]{1,0:T(8,128)(2,1)S(1)}, u32[]{:S(2)}, u32[]{:S(2)}) collective-permute-start(bf16[40,512]{1,0:T(8,128)(2,1)S(1)} %get-tuple-element.17), channel_id=1, source_target_pairs={{256,225},{257,224},{258,227},{259,226},{260,229},{261,228},{262,2... | collective-permute-start | bytes 122888 | tf_op jit(solution)/shard_map/ppermute | solution.py:305
  3.7 6.8 %collective-permute-start = (bf16[32,512]{1,0:T(8,128)(2,1)S(1)}, bf16[32,512]{1,0:T(8,128)(2,1)S(1)}, u32[]{:S(2)}, u32[]{:S(2)}) collective-permute-start(bf16[32,512]{1,0:T(8,128)(2,1)S(1)} %get-tuple-element.14), channel_id=1, source_target_pairs={{1,2},{2,1},{3,4},{4,3},{5,6},{6,5},{7,8},{8,7},{9,10},{10,9},{11,... | collective-permute-start | bytes 98312 | tf_op jit(solution)/shard_map/ppermute | solution.py:310
  8.5 4.7 %collective-permute-start.1 = (bf16[32,512]{1,0:T(8,128)(2,1)S(1)}, bf16[32,512]{1,0:T(8,128)(2,1)S(1)}, u32[]{:S(2)}, u32[]{:S(2)}) collective-permute-start(bf16[32,512]{1,0:T(8,128)(2,1)S(1)} %get-tuple-element.15), channel_id=1, source_target_pairs={{0,1},{1,0},{2,3},{3,2},{4,5},{5,4},{6,7},{7,6},{8,9},{9,8},{10,11... | collective-permute-start | bytes 98312 | tf_op jit(solution)/shard_map/ppermute | solution.py:311
  13.7 13.9 %collective-permute-start.2 = (bf16[160,512]{1,0:T(8,128)(2,1)S(1)}, bf16[160,512]{1,0:T(8,128)(2,1)S(1)}, u32[]{:S(2)}, u32[]{:S(2)}) collective-permute-start(bf16[160,512]{1,0:T(8,128)(2,1)S(1)} %shard_map.38.own_ref), channel_id=1, source_target_pairs={{32,0},{64,32},{96,64},{128,96},{160,128},{192,160},{224,192},{288... | collective-permute-start | bytes 491528 | tf_op jit(solution)/shard_map/ppermute | solution.py:313

commit v4 on v3

--- a/solution.py
+++ b/solution.py
@@ -49,19 +49,19 @@
     return s16[:rows] + s[SIDE - 1 : SIDE - 1 + rows]
 
 
-def normalized(x, tissue, g):
-    rows = tissue.shape[0]
-    xf = x
-    x = xf.astype(BF16)
-    sq = xf * xf
+def standardized(x, rows, g):
+    sq = x * x
     sq_hi = sq.astype(BF16)
     sq_lo = (sq - sq_hi.astype(F32)).astype(BF16)
     area = 1.0 / float(SIDE * SIDE)
-    mean = down(across(x, g), rows) * area
+    mean = down(across(x.astype(BF16), g), rows) * area
     square = down(across(sq_hi, g) + across(sq_lo, g), rows) * area
     var = jnp.maximum(square - mean * mean, 0.0)
-    scaled = (xf[BOX : BOX + rows] - mean) * lax.rsqrt(var + EPSILON)
-    return (tissue * scaled).astype(BF16)
+    return (x[BOX : BOX + rows] - mean) * lax.rsqrt(var + EPSILON)
+
+
+def normalized(x, tissue, g):
+    return (tissue * standardized(x, tissue.shape[0], g)).astype(BF16)
 
 
 def shifted(a, valid, lhs, own_scale):
@@ -168,6 +168,7 @@
 SLAB = RIM + 2 * BOX
 FAR_SLAB = 40
 FAR = 7
+EARLY = 16
 PARAMS = pltpu.CompilerParams(vmem_limit_bytes=48 << 20)
 LONG = pl.CostEstimate(flops=1 << 33, bytes_accessed=1 << 20, transcendentals=0)
 SHORT = pl.CostEstimate(flops=1, bytes_accessed=1, transcendentals=0)
@@ -184,11 +185,15 @@
     ]
     for copy in copies:
         copy.start()
-    for copy in copies:
-        copy.wait()
+    g = band()
+    patch = iota((8, 64 * PCOL), 1) // 64
+    copies[0].wait()
     x = image[...].astype(F32)
+    scaled = standardized(x, INNER, g)
+    copies[1].wait()
+    copies[2].wait()
     marks = tissue[...].astype(F32)
-    inner = normalized(x, marks[BOX : PATCH - BOX], band())
+    inner = (marks[BOX : PATCH - BOX] * scaled).astype(BF16)
     top, bottom = x[:RIM], x[PATCH - RIM :]
     top_marks, bottom_marks = marks[:BOX], marks[PATCH - BOX :]
     core_ref[:INNER] = inner
@@ -196,7 +201,6 @@
     inner = inner.astype(F32)
     upper = jnp.concatenate([inner[:BOX], top, top_marks], axis=0).astype(BF16)
     lower = jnp.concatenate([inner[INNER - BOX :], bottom, bottom_marks], axis=0).astype(BF16)
-    patch = iota((8, 64 * PCOL), 1) // 64
     valid = jnp.zeros((8, 64 * PCOL), jnp.int32)
     for p in range(PCOL):
         valid = jnp.where(patch == p, flags[p], valid)
@@ -234,8 +238,22 @@
     return jnp.concatenate([low[:BOX], above, core[:INNER], below, high[:BOX]], axis=0)
 
 
-def complete_body(core_ref, first_ref, second_ref, out_ref):
-    out_ref[...] = completed(core_ref[...], first_ref[...], second_ref[...]).astype(BF16)
+def complete_body(core_ref, first_ref, second_ref, early_first_ref, early_second_ref, out_ref):
+    first = first_ref[...].astype(F32) + early_first_ref[...].astype(F32)
+    second = second_ref[...].astype(F32) + early_second_ref[...].astype(F32)
+    out_ref[...] = completed(core_ref[...], first, second).astype(BF16)
+
+
+def choose_body(core_ref, first_ref, second_ref, out_ref):
+    ready = (lax.axis_index("sec") == FAR + 1) & (lax.axis_index("xy") >= EARLY)
+
+    @pl.when(ready)
+    def _():
+        out_ref[...] = completed(core_ref[...], first_ref[...], second_ref[...]).astype(BF16)
+
+    @pl.when(jnp.logical_not(ready))
+    def _():
+        out_ref[...] = core_ref[...]
 
 
 def shifted_body(own_ref, valid_ref, lhs_ref, own_scale_ref):
@@ -247,9 +265,15 @@
 
 
 def far_body(core_ref, first_ref, second_ref, own_scale_ref, out_ref):
-    @pl.when(is_far())
+    early = lax.axis_index("xy") < EARLY
+
+    @pl.when(is_far() & early)
     def _():
         out_ref[...] = completed(core_ref[...], first_ref[:SLAB], second_ref[:SLAB]).astype(BF16)
+
+    @pl.when(is_far() & jnp.logical_not(early))
+    def _():
+        out_ref[...] = core_ref[...]
 
 
 def correlate_body(next_ref, far_ref, lhs_ref, own_scale_ref, out_ref, *scratch):
@@ -300,16 +324,27 @@
         ],
     )
 
+    def swap(block, pairs, keep):
+        route = [(s * strips + a, s * strips + b) for s in range(sections) for a, b in pairs if keep(s, a, b)]
+        return lax.ppermute(block, ("sec", "xy"), route)
+
     def from_far(block, pairs):
         route = [((FAR + 1) * strips + a, FAR * strips + b) for a, b in pairs]
         return lax.ppermute(block, ("sec", "xy"), route)
 
-    core_far = from_far(core, [(i, i) for i in range(strips)])
-    first_far = from_far(first_far, odd)
-    second_far = from_far(second_far, even)
-    first = lax.ppermute(first, "xy", odd)
-    second = lax.ppermute(second, "xy", even)
-    own = call(complete_body, rows(EXT), (core, first, second), cost=SHORT)
+    def ahead(s, a, b):
+        return s == FAR + 1 and b >= EARLY
+
+    def rest(s, a, b):
+        return not ahead(s, a, b)
+
+    early_first, early_second = swap(first, odd, ahead), swap(second, even, ahead)
+    chosen = call(choose_body, rows(EXT), (core, early_first, early_second), cost=SHORT)
+    core_far = from_far(chosen, [(i, i) for i in range(strips)])
+    first_far = from_far(first_far, [(a, b) for a, b in odd if b < EARLY])
+    second_far = from_far(second_far, [(a, b) for a, b in even if b < EARLY])
+    first, second = swap(first, odd, rest), swap(second, even, rest)
+    own = call(complete_body, rows(EXT), (core, first, second, early_first, early_second), cost=SHORT)
     following = lax.ppermute(own, "sec", [(s + 1, s) for s in range(sections - 1) if s != FAR])
     lhs, own_scale = call(
         shifted_body,

time: 30.7 us -> 30.3 us (0.987)
  the two profiles are of different devices: /device:TPU:481 before, /device:TPU:185 now
where the time goes in v4:
time: 30.3 us; the launch traced here: 30 us
  starting transfers between devices  13.6 us (45%)
  waiting for transfers between devices  9.86 us (33%)
  Pallas kernels  6.45 us (21%)
    ppermute x4, starting transfers between devices, swap(): return lax.ppermute(block, ('sec', 'xy'), route)  7.58 us
    ppermute x3, waiting for transfers between devices, from_far(): return lax.ppermute(block, ('sec', 'xy'), route)  7.51 us
    pallas_call x6, Pallas kernels, call(): pl.pallas_call(body, out_shape=out_shape, in_specs=in_specs or [VMEM] * l...  6.45 us
    ppermute x1, starting transfers between devices, shards(): lax.ppermute(own, 'sec', [(s + 1, s) for s in range(sections - 1) if s !=...  3.39 us
    ppermute x3, starting transfers between devices, from_far(): return lax.ppermute(block, ('sec', 'xy'), route)  2.62 us
    ppermute x4, waiting for transfers between devices, swap(): return lax.ppermute(block, ('sec', 'xy'), route)  2.35 us
  transfers between devices with their start and end apart: 8, of which 3 were waited for; matrix products, arithmetic and copies ran while one was open for 0% of the time, Pallas kernels for 7%

profile of v4, /device:TPU:185, one launch (start us, length us, event | category | flops | bytes accessed | tf_op | source)
XLA Modules:
  0.0 30.0 jit_solution(12816663318445677220)
XLA Ops:
  0.0 1.5 %shard_map.37 = (bf16[160,512]{1,0:T(8,128)(2,1)S(1)}, bf16[32,512]{1,0:T(8,128)(2,1)S(1)}, bf16[32,512]{1,0:T(8,128)(2,1)S(1)}, bf16[40,512]{1,0:T(8,128)(2,1)S...) custom-call(bf16[128,512]{1,0:T(8,128)(2,1)} %bitcast.5, s32[128,512]{1,0:T(8,128)} %bitcast.4, s32[4]{0:T(128)} %bitcast.6), custom_call_target="tpu_custom_call" | custom-call | tf_op jit(solution)/shard_map/pallas_call | solution.py:294
  1.5 0.7 %collective-permute-start.2 = (bf16[32,512]{1,0:T(8,128)(2,1)S(1)}, bf16[32,512]{1,0:T(8,128)(2,1)S(1)}, u32[]{:S(2)}, u32[]{:S(2)}) collective-permute-start(bf16[32,512]{1,0:T(8,128)(2,1)S(1)} %get-tuple-element.14), channel_id=1, source_target_pairs={{271,272},{273,274},{274,273},{275,276},{276,275},{277,278},{278,2... | collective-permute-start | bytes 98312 | tf_op jit(solution)/shard_map/ppermute | solution.py:329
  2.1 0.7 %collective-permute-start.3 = (bf16[32,512]{1,0:T(8,128)(2,1)S(1)}, bf16[32,512]{1,0:T(8,128)(2,1)S(1)}, u32[]{:S(2)}, u32[]{:S(2)}) collective-permute-start(bf16[32,512]{1,0:T(8,128)(2,1)S(1)} %get-tuple-element.15), channel_id=1, source_target_pairs={{272,273},{273,272},{274,275},{275,274},{276,277},{277,276},{278,2... | collective-permute-start | bytes 98312 | tf_op jit(solution)/shard_map/ppermute | solution.py:329
  2.8 0.0 collective-permute-done.2.early_first_ref.first_ref
  2.8 0.0 collective-permute-done.3.early_second_ref.second_ref
  2.9 1.3 %collective-permute-start.5 = (bf16[160,512]{1,0:T(8,128)(2,1)S(1)}, bf16[160,512]{1,0:T(8,128)(2,1)S(1)}, u32[]{:S(2)}, u32[]{:S(2)}) collective-permute-start(bf16[160,512]{1,0:T(8,128)(2,1)S(1)} %shard_map.39), channel_id=1, source_target_pairs={{256,224},{257,225},{258,226},{259,227},{260,228},{261,229},{262,2... | collective-permute-start | bytes 491528 | tf_op jit(solution)/shard_map/ppermute | solution.py:333
  4.2 0.7 %collective-permute-start.6 = (bf16[40,512]{1,0:T(8,128)(2,1)S(1)}, bf16[40,512]{1,0:T(8,128)(2,1)S(1)}, u32[]{:S(2)}, u32[]{:S(2)}) collective-permute-start(bf16[40,512]{1,0:T(8,128)(2,1)S(1)} %get-tuple-element.16), channel_id=1, source_target_pairs={{257,226},{258,225},{259,228},{260,227},{261,230},{262,229},{263,2... | collective-permute-start | bytes 122888 | tf_op jit(solution)/shard_map/ppermute | solution.py:333
  4.8 0.7 %collective-permute-start.7 = (bf16[40,512]{1,0:T(8,128)(2,1)S(1)}, bf16[40,512]{1,0:T(8,128)(2,1)S(1)}, u32[]{:S(2)}, u32[]{:S(2)}) collective-permute-start(bf16[40,512]{1,0:T(8,128)(2,1)S(1)} %get-tuple-element.17), channel_id=1, source_target_pairs={{256,225},{257,224},{258,227},{259,226},{260,229},{261,228},{262,2... | collective-permute-start | bytes 122888 | tf_op jit(solution)/shard_map/ppermute | solution.py:333
  5.5 3.9 %collective-permute-start = (bf16[32,512]{1,0:T(8,128)(2,1)S(1)}, bf16[32,512]{1,0:T(8,128)(2,1)S(1)}, u32[]{:S(2)}, u32[]{:S(2)}) collective-permute-start(bf16[32,512]{1,0:T(8,128)(2,1)S(1)} %get-tuple-element.14), channel_id=1, source_target_pairs={{1,2},{2,1},{3,4},{4,3},{5,6},{6,5},{7,8},{8,7},{9,10},{10,9},{11,... | collective-permute-start | bytes 98312 | tf_op jit(solution)/shard_map/ppermute | solution.py:329
  9.5 2.3 %collective-permute-start.1 = (bf16[32,512]{1,0:T(8,128)(2,1)S(1)}, bf16[32,512]{1,0:T(8,128)(2,1)S(1)}, u32[]{:S(2)}, u32[]{:S(2)}) collective-permute-start(bf16[32,512]{1,0:T(8,128)(2,1)S(1)} %get-tuple-element.15), channel_id=1, source_target_pairs={{0,1},{1,0},{2,3},{3,2},{4,5},{5,4},{6,7},{7,6},{8,9},{9,8},{10,11... | collective-permute-start | bytes 98312 | tf_op jit(solution)/shard_map/ppermute | solution.py:329
  11.8 0.5 %collective-permute-done.first_ref = bf16[32,512]{1,0:T(8,128)(2,1)S(1)} collective-permute-done((bf16[32,512]{1,0:T(8,128)(2,1)S(1)}, bf16[32,512]{1,0:T(8,128)(2,1)S(1)}, u32[]{:S(2)}, u32[]{:S(2)}) %collective-permute-start) | collective-permute-done | bytes 32800 | tf_op jit(solution)/shard_map/ppermute | solution.py:329
  12.3 1.8 %collective-permute-done.1.second_ref = bf16[32,512]{1,0:T(8,128)(2,1)S(1)} collective-permute-done((bf16[32,512]{1,0:T(8,128)(2,1)S(1)}, bf16[32,512]{1,0:T(8,128)(2,1)S(1)}, u32[]{:S(2)}, u32[]{:S(2)}) %collective-permute-start.1) | collective-permute-done | bytes 32800 | tf_op jit(solution)/shard_map/ppermute | solution.py:329
  14.1 0.5 %shard_map.38.own_ref = bf16[160,512]{1,0:T(8,128)(2,1)S(1)} custom-call(bf16[160,512]{1,0:T(8,128)(2,1)S(1)} %get-tuple-element.13.core_ref, bf16[32,512]{1,0:T(8,128)(2,1)S(1)} %collective-permute-done.first_ref, bf16[32,512]{1,0:T(8,128)(2,1)S(1)} %collective-permute-done.1.second_ref, ...), custom_call_target="tpu_custom_call" | custom-call | flops 1 | bytes 1 | tf_op jit(solution)/shard_map/pallas_call | solution.py:294
  14.6 3.4 %collective-permute-start.4 = (bf16[160,512]{1,0:T(8,128)(2,1)S(1)}, bf16[160,512]{1,0:T(8,128)(2,1)S(1)}, u32[]{:S(2)}, u32[]{:S(2)}) collective-permute-start(bf16[160,512]{1,0:T(8,128)(2,1)S(1)} %shard_map.38.own_ref), channel_id=1, source_target_pairs={{32,0},{64,32},{96,64},{128,96},{160,128},{192,160},{224,192},{288... | collective-permute-start | bytes 491528 | tf_op jit(solution)/shard_map/ppermute | solution.py:348
  18.0 1.5 %shard_map.40 = (bf16[1056,2560]{1,0:T(8,128)(2,1)S(1)}, f32[8,256]{1,0:T(8,128)S(1)}) custom-call(bf16[160,512]{1,0:T(8,128)(2,1)S(1)} %shard_map.38.own_ref, f32[8,256]{1,0:T(8,128)S(1)} %get-tuple-element.18.valid_ref), custom_call_target="tpu_custom_call" | custom-call | flops 1 | bytes 1 | tf_op jit(solution)/shard_map/pallas_call | solution.py:294
  19.6 0.0 collective-permute-done.6.first_ref
  19.6 0.0 collective-permute-done.7.second_ref
  19.6 7.5 %collective-permute-done.5.core_ref = bf16[160,512]{1,0:T(8,128)(2,1)S(1)} collective-permute-done((bf16[160,512]{1,0:T(8,128)(2,1)S(1)}, bf16[160,512]{1,0:T(8,128)(2,1)S(1)}, u32[]{:S(2)}, u32[]{:S(2)}) %collective-permute-start.5) | collective-permute-done | bytes 163872 | tf_op jit(solution)/shard_map/ppermute | solution.py:333
  27.1 0.0 collective-permute-done.4.next_ref
  27.1 2.9 %shard_map.42 = f32[4,1089]{1,0:T(4,128)} custom-call(bf16[160,512]{1,0:T(8,128)(2,1)S(1)} %collective-permute-done.4.next_ref, bf16[160,512]{1,0:T(8,128)(2,1)S(1)} %shard_map.41.far_ref, bf16[1056,2560]{1,0:T(8,128)(2,1)S(1)} %get-tuple-element.20.lhs_ref, f32[8,256]{1,0:T(8,128)S(1)} %get-tuple-element.19.own_scale_ref), custom_call_target="tpu_custom_call" | custom-call | tf_op jit(solution)/shard_map/pallas_call | solution.py:294
  (2 shorter events, 0.0 us)
Async XLA Ops:
  1.5 1.3 %collective-permute-start.2 = (bf16[32,512]{1,0:T(8,128)(2,1)S(1)}, bf16[32,512]{1,0:T(8,128)(2,1)S(1)}, u32[]{:S(2)}, u32[]{:S(2)}) collective-permute-start(bf16[32,512]{1,0:T(8,128)(2,1)S(1)} %get-tuple-element.14), channel_id=1, source_target_pairs={{271,272},{273,274},{274,273},{275,276},{276,275},{277,278},{278,2... | collective-permute-start | bytes 98312 | tf_op jit(solution)/shard_map/ppermute | solution.py:329
  2.1 0.7 %collective-permute-start.3 = (bf16[32,512]{1,0:T(8,128)(2,1)S(1)}, bf16[32,512]{1,0:T(8,128)(2,1)S(1)}, u32[]{:S(2)}, u32[]{:S(2)}) collective-permute-start(bf16[32,512]{1,0:T(8,128)(2,1)S(1)} %get-tuple-element.15), channel_id=1, source_target_pairs={{272,273},{273,272},{274,275},{275,274},{276,277},{277,276},{278,2... | collective-permute-start | bytes 98312 | tf_op jit(solution)/shard_map/ppermute | solution.py:329
  2.9 24.2 %collective-permute-start.5 = (bf16[160,512]{1,0:T(8,128)(2,1)S(1)}, bf16[160,512]{1,0:T(8,128)(2,1)S(1)}, u32[]{:S(2)}, u32[]{:S(2)}) collective-permute-start(bf16[160,512]{1,0:T(8,128)(2,1)S(1)} %shard_map.39), channel_id=1, source_target_pairs={{256,224},{257,225},{258,226},{259,227},{260,228},{261,229},{262,2... | collective-permute-start | bytes 491528 | tf_op jit(solution)/shard_map/ppermute | solution.py:333
  4.2 15.4 %collective-permute-start.6 = (bf16[40,512]{1,0:T(8,128)(2,1)S(1)}, bf16[40,512]{1,0:T(8,128)(2,1)S(1)}, u32[]{:S(2)}, u32[]{:S(2)}) collective-permute-start(bf16[40,512]{1,0:T(8,128)(2,1)S(1)} %get-tuple-element.16), channel_id=1, source_target_pairs={{257,226},{258,225},{259,228},{260,227},{261,230},{262,229},{263,2... | collective-permute-start | bytes 122888 | tf_op jit(solution)/shard_map/ppermute | solution.py:333
  4.8 14.7 %collective-permute-start.7 = (bf16[40,512]{1,0:T(8,128)(2,1)S(1)}, bf16[40,512]{1,0:T(8,128)(2,1)S(1)}, u32[]{:S(2)}, u32[]{:S(2)}) collective-permute-start(bf16[40,512]{1,0:T(8,128)(2,1)S(1)} %get-tuple-element.17), channel_id=1, source_target_pairs={{256,225},{257,224},{258,227},{259,226},{260,229},{261,228},{262,2... | collective-permute-start | bytes 122888 | tf_op jit(solution)/shard_map/ppermute | solution.py:333
  5.5 6.8 %collective-permute-start = (bf16[32,512]{1,0:T(8,128)(2,1)S(1)}, bf16[32,512]{1,0:T(8,128)(2,1)S(1)}, u32[]{:S(2)}, u32[]{:S(2)}) collective-permute-start(bf16[32,512]{1,0:T(8,128)(2,1)S(1)} %get-tuple-element.14), channel_id=1, source_target_pairs={{1,2},{2,1},{3,4},{4,3},{5,6},{6,5},{7,8},{8,7},{9,10},{10,9},{11,... | collective-permute-start | bytes 98312 | tf_op jit(solution)/shard_map/ppermute | solution.py:329
  9.5 4.7 %collective-permute-start.1 = (bf16[32,512]{1,0:T(8,128)(2,1)S(1)}, bf16[32,512]{1,0:T(8,128)(2,1)S(1)}, u32[]{:S(2)}, u32[]{:S(2)}) collective-permute-start(bf16[32,512]{1,0:T(8,128)(2,1)S(1)} %get-tuple-element.15), channel_id=1, source_target_pairs={{0,1},{1,0},{2,3},{3,2},{4,5},{5,4},{6,7},{7,6},{8,9},{9,8},{10,11... | collective-permute-start | bytes 98312 | tf_op jit(solution)/shard_map/ppermute | solution.py:329
  14.6 12.5 %collective-permute-start.4 = (bf16[160,512]{1,0:T(8,128)(2,1)S(1)}, bf16[160,512]{1,0:T(8,128)(2,1)S(1)}, u32[]{:S(2)}, u32[]{:S(2)}) collective-permute-start(bf16[160,512]{1,0:T(8,128)(2,1)S(1)} %shard_map.38.own_ref), channel_id=1, source_target_pairs={{32,0},{64,32},{96,64},{128,96},{160,128},{192,160},{224,192},{288... | collective-permute-start | bytes 491528 | tf_op jit(solution)/shard_map/ppermute | solution.py:348

commit v5 on v4

--- a/solution.py
+++ b/solution.py
@@ -49,19 +49,18 @@
     return s16[:rows] + s[SIDE - 1 : SIDE - 1 + rows]
 
 
-def standardized(x, rows, g):
+def sums_across(x, g):
     sq = x * x
     sq_hi = sq.astype(BF16)
     sq_lo = (sq - sq_hi.astype(F32)).astype(BF16)
+    return across(x.astype(BF16), g), across(sq_hi, g) + across(sq_lo, g)
+
+
+def standardized(x, total, total_sq, rows):
     area = 1.0 / float(SIDE * SIDE)
-    mean = down(across(x.astype(BF16), g), rows) * area
-    square = down(across(sq_hi, g) + across(sq_lo, g), rows) * area
-    var = jnp.maximum(square - mean * mean, 0.0)
+    mean = down(total, rows) * area
+    var = jnp.maximum(down(total_sq, rows) * area - mean * mean, 0.0)
     return (x[BOX : BOX + rows] - mean) * lax.rsqrt(var + EPSILON)
-
-
-def normalized(x, tissue, g):
-    return (tissue * standardized(x, tissue.shape[0], g)).astype(BF16)
 
 
 def shifted(a, valid, lhs, own_scale):
@@ -168,14 +167,14 @@
 SLAB = RIM + 2 * BOX
 FAR_SLAB = 40
 FAR = 7
-EARLY = 16
+EARLY = 20
 PARAMS = pltpu.CompilerParams(vmem_limit_bytes=48 << 20)
 LONG = pl.CostEstimate(flops=1 << 33, bytes_accessed=1 << 20, transcendentals=0)
 SHORT = pl.CostEstimate(flops=1, bytes_accessed=1, transcendentals=0)
 
 
 def prepare_body(
-    image_hbm, tissue_hbm, flags_hbm, core_ref, first_ref, second_ref, first_far_ref, second_far_ref, valid_ref,
+    image_hbm, tissue_hbm, flags_hbm, core_ref, first_ref, second_ref, first_far_ref, second_far_ref, valid_ref, band_ref,
     image, tissue, flags, sems,
 ):
     copies = [
@@ -186,10 +185,11 @@
     for copy in copies:
         copy.start()
     g = band()
+    band_ref[...] = g
     patch = iota((8, 64 * PCOL), 1) // 64
     copies[0].wait()
     x = image[...].astype(F32)
-    scaled = standardized(x, INNER, g)
+    scaled = standardized(x, *sums_across(x, g), INNER)
     copies[1].wait()
     copies[2].wait()
     marks = tissue[...].astype(F32)
@@ -222,34 +222,33 @@
         second_far_ref[:SLAB] = upper
 
 
-def completed(core, first, second):
+def completed(core, first, second, g):
     keep = jnp.where(lax.axis_index("xy") % 2 == 0, 1.0, 0.0).astype(F32)
     core, first, second = core.astype(F32), first.astype(F32), second.astype(F32)
     low = first * keep + second * (1.0 - keep)
     high = second * keep + first * (1.0 - keep)
     edges = core[INNER:]
-    g = band()
-    x = jnp.concatenate([low[BOX : BOX + RIM], edges[:RIM]], axis=0)
-    tissue = jnp.concatenate([low[BOX + RIM :], edges[2 * RIM : 2 * RIM + BOX]], axis=0)
-    above = normalized(x, tissue, g).astype(F32)
-    x = jnp.concatenate([edges[RIM : 2 * RIM], high[BOX : BOX + RIM]], axis=0)
-    tissue = jnp.concatenate([edges[2 * RIM + BOX :], high[BOX + RIM :]], axis=0)
-    below = normalized(x, tissue, g).astype(F32)
+    x = jnp.concatenate([low[BOX : BOX + RIM], edges[: 2 * RIM], high[BOX : BOX + RIM]], axis=0)
+    total, total_sq = sums_across(x, g)
+    marks = edges[2 * RIM :]
+    n = 2 * RIM
+    above = jnp.concatenate([low[BOX + RIM :], marks[:BOX]], axis=0) * standardized(x[:n], total[:n], total_sq[:n], RIM)
+    below = jnp.concatenate([marks[BOX:], high[BOX + RIM :]], axis=0) * standardized(x[n:], total[n:], total_sq[n:], RIM)
     return jnp.concatenate([low[:BOX], above, core[:INNER], below, high[:BOX]], axis=0)
 
 
-def complete_body(core_ref, first_ref, second_ref, early_first_ref, early_second_ref, out_ref):
+def complete_body(core_ref, first_ref, second_ref, early_first_ref, early_second_ref, band_ref, out_ref):
     first = first_ref[...].astype(F32) + early_first_ref[...].astype(F32)
     second = second_ref[...].astype(F32) + early_second_ref[...].astype(F32)
-    out_ref[...] = completed(core_ref[...], first, second).astype(BF16)
-
-
-def choose_body(core_ref, first_ref, second_ref, out_ref):
+    out_ref[...] = completed(core_ref[...], first, second, band_ref[...]).astype(BF16)
+
+
+def choose_body(core_ref, first_ref, second_ref, band_ref, out_ref):
     ready = (lax.axis_index("sec") == FAR + 1) & (lax.axis_index("xy") >= EARLY)
 
     @pl.when(ready)
     def _():
-        out_ref[...] = completed(core_ref[...], first_ref[...], second_ref[...]).astype(BF16)
+        out_ref[...] = completed(core_ref[...], first_ref[...], second_ref[...], band_ref[...]).astype(BF16)
 
     @pl.when(jnp.logical_not(ready))
     def _():
@@ -264,12 +263,12 @@
     return lax.axis_index("sec") == FAR
 
 
-def far_body(core_ref, first_ref, second_ref, own_scale_ref, out_ref):
+def far_body(core_ref, first_ref, second_ref, own_scale_ref, band_ref, out_ref):
     early = lax.axis_index("xy") < EARLY
 
     @pl.when(is_far() & early)
     def _():
-        out_ref[...] = completed(core_ref[...], first_ref[:SLAB], second_ref[:SLAB]).astype(BF16)
+        out_ref[...] = completed(core_ref[...], first_ref[:SLAB], second_ref[:SLAB], band_ref[...]).astype(BF16)
 
     @pl.when(is_far() & jnp.logical_not(early))
     def _():
@@ -311,9 +310,9 @@
     def rows(count):
         return jax.ShapeDtypeStruct((count, W), BF16)
 
-    core, first, second, first_far, second_far, valid = call(
+    core, first, second, first_far, second_far, valid, bands = call(
         prepare_body,
-        (rows(PATCH + 2 * RIM), rows(SLAB), rows(SLAB), rows(FAR_SLAB), rows(FAR_SLAB), jax.ShapeDtypeStruct((8, 64 * PCOL), F32)),
+        (rows(PATCH + 2 * RIM), rows(SLAB), rows(SLAB), rows(FAR_SLAB), rows(FAR_SLAB), jax.ShapeDtypeStruct((8, 64 * PCOL), F32), jax.ShapeDtypeStruct((W, W // 2), BF16)),
         tuple(pltpu.with_memory_space_constraint(x, pltpu.HBM) for x in (image, mask, flags)),
         in_specs=[pl.BlockSpec(memory_space=pltpu.HBM)] * 3,
         scratch=[
@@ -339,12 +338,12 @@
         return not ahead(s, a, b)
 
     early_first, early_second = swap(first, odd, ahead), swap(second, even, ahead)
-    chosen = call(choose_body, rows(EXT), (core, early_first, early_second), cost=SHORT)
+    chosen = call(choose_body, rows(EXT), (core, early_first, early_second, bands), cost=SHORT)
     core_far = from_far(chosen, [(i, i) for i in range(strips)])
     first_far = from_far(first_far, [(a, b) for a, b in odd if b < EARLY])
     second_far = from_far(second_far, [(a, b) for a, b in even if b < EARLY])
     first, second = swap(first, odd, rest), swap(second, even, rest)
-    own = call(complete_body, rows(EXT), (core, first, second, early_first, early_second), cost=SHORT)
+    own = call(complete_body, rows(EXT), (core, first, second, early_first, early_second, bands), cost=SHORT)
     following = lax.ppermute(own, "sec", [(s + 1, s) for s in range(sections - 1) if s != FAR])
     lhs, own_scale = call(
         shifted_body,
@@ -355,7 +354,7 @@
         (own, valid),
         cost=SHORT,
     )
-    far = call(far_body, rows(EXT), (core_far, first_far, second_far, own_scale), cost=LONG)
+    far = call(far_body, rows(EXT), (core_far, first_far, second_far, own_scale, bands), cost=LONG)
     scores = call(
         correlate_body,
         jax.ShapeDtypeStruct((PCOL, SPAN * SPAN), F32),

time: 30.3 us -> 30.2 us (level)
  the two profiles are of different devices: /device:TPU:185 before, /device:TPU:217 now
where the time goes in v5:
time: 30.2 us; the launch traced here: 29.9 us
  starting transfers between devices  13.6 us (45%)
  waiting for transfers between devices  9.86 us (33%)
  Pallas kernels  6.34 us (21%)
    ppermute x4, starting transfers between devices, swap(): return lax.ppermute(block, ('sec', 'xy'), route)  7.57 us
    ppermute x3, waiting for transfers between devices, from_far(): return lax.ppermute(block, ('sec', 'xy'), route)  7.51 us
    pallas_call x6, Pallas kernels, call(): pl.pallas_call(body, out_shape=out_shape, in_specs=in_specs or [VMEM] * l...  6.34 us
    ppermute x1, starting transfers between devices, shards(): lax.ppermute(own, 'sec', [(s + 1, s) for s in range(sections - 1) if s !=...  3.39 us
    ppermute x3, starting transfers between devices, from_far(): return lax.ppermute(block, ('sec', 'xy'), route)  2.62 us
    ppermute x4, waiting for transfers between devices, swap(): return lax.ppermute(block, ('sec', 'xy'), route)  2.35 us
  transfers between devices with their start and end apart: 8, of which 3 were waited for; matrix products, arithmetic and copies ran while one was open for 0% of the time, Pallas kernels for 6%

profile of v5, /device:TPU:217, one launch (start us, length us, event | category | flops | bytes accessed | tf_op | source)
XLA Modules:
  0.0 29.9 jit_solution(4424059043008071332)
XLA Ops:
  0.0 1.5 %shard_map.37 = (bf16[160,512]{1,0:T(8,128)(2,1)S(1)}, bf16[32,512]{1,0:T(8,128)(2,1)S(1)}, bf16[32,512]{1,0:T(8,128)(2,1)S(1)}, bf16[40,512]{1,0:T(8,128)(2,1)S...) custom-call(bf16[128,512]{1,0:T(8,128)(2,1)} %bitcast.5, ...), custom_call_target="tpu_custom_call" | custom-call | tf_op jit(solution)/shard_map/pallas_call | solution.py:293
  1.5 0.7 %collective-permute-start.2 = (bf16[32,512]{1,0:T(8,128)(2,1)S(1)}, bf16[32,512]{1,0:T(8,128)(2,1)S(1)}, u32[]{:S(2)}, u32[]{:S(2)}) collective-permute-start(bf16[32,512]{1,0:T(8,128)(2,1)S(1)} %get-tuple-element.15), channel_id=1, source_target_pairs={{275,276},{277,278},{278,277},{279,280},{280,279},{281,282},{282,2... | collective-permute-start | bytes 98312 | tf_op jit(solution)/shard_map/ppermute | solution.py:328
  2.2 0.7 %collective-permute-start.3 = (bf16[32,512]{1,0:T(8,128)(2,1)S(1)}, bf16[32,512]{1,0:T(8,128)(2,1)S(1)}, u32[]{:S(2)}, u32[]{:S(2)}) collective-permute-start(bf16[32,512]{1,0:T(8,128)(2,1)S(1)} %get-tuple-element.16), channel_id=1, source_target_pairs={{276,277},{277,276},{278,279},{279,278},{280,281},{281,280},{282,2... | collective-permute-start | bytes 98312 | tf_op jit(solution)/shard_map/ppermute | solution.py:328
  2.8 0.0 collective-permute-done.2.early_first_ref.first_ref
  2.8 0.0 collective-permute-done.3.early_second_ref.second_ref
  2.9 1.3 %collective-permute-start.5 = (bf16[160,512]{1,0:T(8,128)(2,1)S(1)}, bf16[160,512]{1,0:T(8,128)(2,1)S(1)}, u32[]{:S(2)}, u32[]{:S(2)}) collective-permute-start(bf16[160,512]{1,0:T(8,128)(2,1)S(1)} %shard_map.39), channel_id=1, source_target_pairs={{256,224},{257,225},{258,226},{259,227},{260,228},{261,229},{262,2... | collective-permute-start | bytes 491528 | tf_op jit(solution)/shard_map/ppermute | solution.py:332
  4.2 0.7 %collective-permute-start.6 = (bf16[40,512]{1,0:T(8,128)(2,1)S(1)}, bf16[40,512]{1,0:T(8,128)(2,1)S(1)}, u32[]{:S(2)}, u32[]{:S(2)}) collective-permute-start(bf16[40,512]{1,0:T(8,128)(2,1)S(1)} %get-tuple-element.18), channel_id=1, source_target_pairs={{257,226},{258,225},{259,228},{260,227},{261,230},{262,229},{263,2... | collective-permute-start | bytes 122888 | tf_op jit(solution)/shard_map/ppermute | solution.py:332
  4.9 0.7 %collective-permute-start.7 = (bf16[40,512]{1,0:T(8,128)(2,1)S(1)}, bf16[40,512]{1,0:T(8,128)(2,1)S(1)}, u32[]{:S(2)}, u32[]{:S(2)}) collective-permute-start(bf16[40,512]{1,0:T(8,128)(2,1)S(1)} %get-tuple-element.19), channel_id=1, source_target_pairs={{256,225},{257,224},{258,227},{259,226},{260,229},{261,228},{262,2... | collective-permute-start | bytes 122888 | tf_op jit(solution)/shard_map/ppermute | solution.py:332
  5.5 3.9 %collective-permute-start = (bf16[32,512]{1,0:T(8,128)(2,1)S(1)}, bf16[32,512]{1,0:T(8,128)(2,1)S(1)}, u32[]{:S(2)}, u32[]{:S(2)}) collective-permute-start(bf16[32,512]{1,0:T(8,128)(2,1)S(1)} %get-tuple-element.15), channel_id=1, source_target_pairs={{1,2},{2,1},{3,4},{4,3},{5,6},{6,5},{7,8},{8,7},{9,10},{10,9},{11,... | collective-permute-start | bytes 98312 | tf_op jit(solution)/shard_map/ppermute | solution.py:328
  9.5 2.3 %collective-permute-start.1 = (bf16[32,512]{1,0:T(8,128)(2,1)S(1)}, bf16[32,512]{1,0:T(8,128)(2,1)S(1)}, u32[]{:S(2)}, u32[]{:S(2)}) collective-permute-start(bf16[32,512]{1,0:T(8,128)(2,1)S(1)} %get-tuple-element.16), channel_id=1, source_target_pairs={{0,1},{1,0},{2,3},{3,2},{4,5},{5,4},{6,7},{7,6},{8,9},{9,8},{10,11... | collective-permute-start | bytes 98312 | tf_op jit(solution)/shard_map/ppermute | solution.py:328
  11.8 0.5 %collective-permute-done.first_ref = bf16[32,512]{1,0:T(8,128)(2,1)S(1)} collective-permute-done((bf16[32,512]{1,0:T(8,128)(2,1)S(1)}, bf16[32,512]{1,0:T(8,128)(2,1)S(1)}, u32[]{:S(2)}, u32[]{:S(2)}) %collective-permute-start) | collective-permute-done | bytes 32800 | tf_op jit(solution)/shard_map/ppermute | solution.py:328
  12.3 1.8 %collective-permute-done.1.second_ref = bf16[32,512]{1,0:T(8,128)(2,1)S(1)} collective-permute-done((bf16[32,512]{1,0:T(8,128)(2,1)S(1)}, bf16[32,512]{1,0:T(8,128)(2,1)S(1)}, u32[]{:S(2)}, u32[]{:S(2)}) %collective-permute-start.1) | collective-permute-done | bytes 32800 | tf_op jit(solution)/shard_map/ppermute | solution.py:328
  14.1 0.4 %shard_map.38.own_ref = bf16[160,512]{1,0:T(8,128)(2,1)S(1)} custom-call(bf16[160,512]{1,0:T(8,128)(2,1)S(1)} %get-tuple-element.14.core_ref, bf16[32,512]{1,0:T(8,128)(2,1)S(1)} %collective-permute-done.first_ref, bf16[32,512]{1,0:T(8,128)(2,1)S(1)} %collective-permute-done.1.second_ref, ...), custom_call_target="tpu_custom_call" | custom-call | flops 1 | bytes 1 | tf_op jit(solution)/shard_map/pallas_call | solution.py:293
  14.5 3.4 %collective-permute-start.4 = (bf16[160,512]{1,0:T(8,128)(2,1)S(1)}, bf16[160,512]{1,0:T(8,128)(2,1)S(1)}, u32[]{:S(2)}, u32[]{:S(2)}) collective-permute-start(bf16[160,512]{1,0:T(8,128)(2,1)S(1)} %shard_map.38.own_ref), channel_id=1, source_target_pairs={{32,0},{64,32},{96,64},{128,96},{160,128},{192,160},{224,192},{288... | collective-permute-start | bytes 491528 | tf_op jit(solution)/shard_map/ppermute | solution.py:347
  17.9 1.5 %shard_map.40 = (bf16[1056,2560]{1,0:T(8,128)(2,1)S(1)}, f32[8,256]{1,0:T(8,128)S(1)}) custom-call(bf16[160,512]{1,0:T(8,128)(2,1)S(1)} %shard_map.38.own_ref, f32[8,256]{1,0:T(8,128)S(1)} %get-tuple-element.20.valid_ref), custom_call_target="tpu_custom_call" | custom-call | flops 1 | bytes 1 | tf_op jit(solution)/shard_map/pallas_call | solution.py:293
  19.4 0.0 collective-permute-done.6.first_ref
  19.5 0.0 collective-permute-done.7.second_ref
  19.5 7.5 %collective-permute-done.5.core_ref = bf16[160,512]{1,0:T(8,128)(2,1)S(1)} collective-permute-done((bf16[160,512]{1,0:T(8,128)(2,1)S(1)}, bf16[160,512]{1,0:T(8,128)(2,1)S(1)}, u32[]{:S(2)}, u32[]{:S(2)}) %collective-permute-start.5) | collective-permute-done | bytes 163872 | tf_op jit(solution)/shard_map/ppermute | solution.py:332
  27.0 0.0 collective-permute-done.4.next_ref
  27.0 2.9 %shard_map.42 = f32[4,1089]{1,0:T(4,128)} custom-call(bf16[160,512]{1,0:T(8,128)(2,1)S(1)} %collective-permute-done.4.next_ref, bf16[160,512]{1,0:T(8,128)(2,1)S(1)} %shard_map.41.far_ref, bf16[1056,2560]{1,0:T(8,128)(2,1)S(1)} %get-tuple-element.22.lhs_ref, f32[8,256]{1,0:T(8,128)S(1)} %get-tuple-element.21.own_scale_ref), custom_call_target="tpu_custom_call" | custom-call | tf_op jit(solution)/shard_map/pallas_call | solution.py:293
  (2 shorter events, 0.0 us)
Async XLA Ops:
  1.5 1.3 %collective-permute-start.2 = (bf16[32,512]{1,0:T(8,128)(2,1)S(1)}, bf16[32,512]{1,0:T(8,128)(2,1)S(1)}, u32[]{:S(2)}, u32[]{:S(2)}) collective-permute-start(bf16[32,512]{1,0:T(8,128)(2,1)S(1)} %get-tuple-element.15), channel_id=1, source_target_pairs={{275,276},{277,278},{278,277},{279,280},{280,279},{281,282},{282,2... | collective-permute-start | bytes 98312 | tf_op jit(solution)/shard_map/ppermute | solution.py:328
  2.2 0.7 %collective-permute-start.3 = (bf16[32,512]{1,0:T(8,128)(2,1)S(1)}, bf16[32,512]{1,0:T(8,128)(2,1)S(1)}, u32[]{:S(2)}, u32[]{:S(2)}) collective-permute-start(bf16[32,512]{1,0:T(8,128)(2,1)S(1)} %get-tuple-element.16), channel_id=1, source_target_pairs={{276,277},{277,276},{278,279},{279,278},{280,281},{281,280},{282,2... | collective-permute-start | bytes 98312 | tf_op jit(solution)/shard_map/ppermute | solution.py:328
  2.9 24.1 %collective-permute-start.5 = (bf16[160,512]{1,0:T(8,128)(2,1)S(1)}, bf16[160,512]{1,0:T(8,128)(2,1)S(1)}, u32[]{:S(2)}, u32[]{:S(2)}) collective-permute-start(bf16[160,512]{1,0:T(8,128)(2,1)S(1)} %shard_map.39), channel_id=1, source_target_pairs={{256,224},{257,225},{258,226},{259,227},{260,228},{261,229},{262,2... | collective-permute-start | bytes 491528 | tf_op jit(solution)/shard_map/ppermute | solution.py:332
  4.2 15.3 %collective-permute-start.6 = (bf16[40,512]{1,0:T(8,128)(2,1)S(1)}, bf16[40,512]{1,0:T(8,128)(2,1)S(1)}, u32[]{:S(2)}, u32[]{:S(2)}) collective-permute-start(bf16[40,512]{1,0:T(8,128)(2,1)S(1)} %get-tuple-element.18), channel_id=1, source_target_pairs={{257,226},{258,225},{259,228},{260,227},{261,230},{262,229},{263,2... | collective-permute-start | bytes 122888 | tf_op jit(solution)/shard_map/ppermute | solution.py:332
  4.9 14.6 %collective-permute-start.7 = (bf16[40,512]{1,0:T(8,128)(2,1)S(1)}, bf16[40,512]{1,0:T(8,128)(2,1)S(1)}, u32[]{:S(2)}, u32[]{:S(2)}) collective-permute-start(bf16[40,512]{1,0:T(8,128)(2,1)S(1)} %get-tuple-element.19), channel_id=1, source_target_pairs={{256,225},{257,224},{258,227},{259,226},{260,229},{261,228},{262,2... | collective-permute-start | bytes 122888 | tf_op jit(solution)/shard_map/ppermute | solution.py:332
  5.5 6.8 %collective-permute-start = (bf16[32,512]{1,0:T(8,128)(2,1)S(1)}, bf16[32,512]{1,0:T(8,128)(2,1)S(1)}, u32[]{:S(2)}, u32[]{:S(2)}) collective-permute-start(bf16[32,512]{1,0:T(8,128)(2,1)S(1)} %get-tuple-element.15), channel_id=1, source_target_pairs={{1,2},{2,1},{3,4},{4,3},{5,6},{6,5},{7,8},{8,7},{9,10},{10,9},{11,... | collective-permute-start | bytes 98312 | tf_op jit(solution)/shard_map/ppermute | solution.py:328
  9.5 4.7 %collective-permute-start.1 = (bf16[32,512]{1,0:T(8,128)(2,1)S(1)}, bf16[32,512]{1,0:T(8,128)(2,1)S(1)}, u32[]{:S(2)}, u32[]{:S(2)}) collective-permute-start(bf16[32,512]{1,0:T(8,128)(2,1)S(1)} %get-tuple-element.16), channel_id=1, source_target_pairs={{0,1},{1,0},{2,3},{3,2},{4,5},{5,4},{6,7},{7,6},{8,9},{9,8},{10,11... | collective-permute-start | bytes 98312 | tf_op jit(solution)/shard_map/ppermute | solution.py:328
  14.5 12.5 %collective-permute-start.4 = (bf16[160,512]{1,0:T(8,128)(2,1)S(1)}, bf16[160,512]{1,0:T(8,128)(2,1)S(1)}, u32[]{:S(2)}, u32[]{:S(2)}) collective-permute-start(bf16[160,512]{1,0:T(8,128)(2,1)S(1)} %shard_map.38.own_ref), channel_id=1, source_target_pairs={{32,0},{64,32},{96,64},{128,96},{160,128},{192,160},{224,192},{288... | collective-permute-start | bytes 491528 | tf_op jit(solution)/shard_map/ppermute | solution.py:347
